TPU v7x, 32 devices: a whole 2x2x4 slice. The times are simulated.
32 devices in a mesh: dp: 8 (over z, x), tensor: 4 (over y, core).
Axes of the slice: x: 2, y: 2, z: 4, core: 2. Of those that a mesh axis runs over, the one named last changes fastest.
Arguments:
- inputs: bfloat16 [16384, 768], P(('dp', 'tensor')), may hold values from -6 to 6
- lengths: int32 [32], P('dp'), may hold values from 20 to 512, as said below
- weight_query: bfloat16 [768, 768], P(None, 'tensor'), may hold values from -0.21875 to 0.21875
- bias_query: bfloat16 [768], P('tensor'), may hold values from -3 to 3
- weight_key: bfloat16 [768, 768], P(None, 'tensor'), may hold values from -0.21875 to 0.21875
- weight_value: bfloat16 [768, 768], P(None, 'tensor'), may hold values from -0.21875 to 0.21875
- bias_value: bfloat16 [768], P('tensor'), may hold values from -3 to 3
- weight_out: bfloat16 [768, 768], P('tensor'), may hold values from -1.75 to 1.75
- bias_out: bfloat16 [768], replicated, may hold values from -2 to 2
- weight_in: bfloat16 [768, 3072], P(None, 'tensor'), may hold values from -0.21875 to 0.21875
- bias_in: bfloat16 [3072], P('tensor'), may hold values from -2 to 2
- weight_down: bfloat16 [3072, 768], P('tensor'), may hold values from -0.109375 to 0.109375
- bias_down: bfloat16 [768], replicated, may hold values from -2 to 2
- first_gain: bfloat16 [768], replicated, may hold values from 0.5 to 1.5
- first_shift: bfloat16 [768], replicated, may hold values from -2 to 2
- second_gain: bfloat16 [768], replicated, may hold values from 0.5 to 1.5
- second_shift: bfloat16 [768], replicated, may hold values from -2 to 2
- cotangent: bfloat16 [16384, 768], P(('dp', 'tensor')), may hold values from -6 to 6
Outputs:
- outputs: bfloat16 [16384, 768], P(('dp', 'tensor'))
- grad_inputs: float32 [16384, 768], P(('dp', 'tensor'))
- grad_weight_query: float32 [768, 768], P(None, 'tensor')
- grad_bias_query: float32 [768], P('tensor')
- grad_weight_key: float32 [768, 768], P(None, 'tensor')
- grad_weight_value: float32 [768, 768], P(None, 'tensor')
- grad_bias_value: float32 [768], P('tensor')
- grad_weight_out: float32 [768, 768], P('tensor')
- grad_bias_out: float32 [768], replicated
- grad_weight_in: float32 [768, 3072], P(None, 'tensor')
- grad_bias_in: float32 [3072], P('tensor')
- grad_weight_down: float32 [3072, 768], P('tensor')
- grad_bias_down: float32 [768], replicated
- grad_first_gain: float32 [768], replicated
- grad_first_shift: float32 [768], replicated
- grad_second_gain: float32 [768], replicated
- grad_second_shift: float32 [768], replicated
Inputs may be any that keep to these rules, and one draw needn't show every extreme that they name: `lengths`: some passage has 512 tokens and some has 20.
All inputs are finite; a program needn't handle non-finite values.
Results may differ from a plain program's by a relative error of at most 0.017.
Values may be sent and summed in bfloat16 or wider, within the bound.
No kernel may reach another device: no remote copies, remote signals or barrier semaphores. Data moves between devices by JAX's collectives and lax.ppermute only.
A program may use at most 128 MiB of HBM per device.

v0:
```python
import math

import jax
import jax.numpy as jnp
from jax import lax
from jax.sharding import PartitionSpec as P

HEAD = 64
SEQ_LEN = 512


def layer_norm(values, gain, shift):
    center = values - jnp.mean(values, axis=-1, keepdims=True)
    spread = jnp.mean(center * center, axis=-1, keepdims=True)
    return center * lax.rsqrt(spread + 1e-12) * gain + shift


def gelu_exact(values):
    return jax.nn.gelu(values, approximate=False)


def contract_rows(left, right):
    return lax.dot_general(
        left, right, (((0,), (0,)), ((), ())), preferred_element_type=jnp.float32
    )


def contract_cols(left, right):
    return lax.dot_general(
        left, right, (((1,), (1,)), ((), ())), preferred_element_type=jnp.float32
    )


def masked_scores(queries, keys_all, length):
    factor = 1.0 / math.sqrt(queries.shape[-1])
    scores = (
        jnp.einsum("qhd,khd->hqk", queries, keys_all, preferred_element_type=jnp.float32) * factor
    )
    visible = lax.broadcasted_iota(jnp.int32, (1, 1, scores.shape[-1]), 2) < length
    return jnp.where(visible, scores, -1e30)


def attend_forward(pieces):
    queries, keys_all, values_all, length = pieces
    scores = masked_scores(queries, keys_all, length)
    highest = jnp.max(scores, axis=-1, keepdims=True)
    exponent = jnp.exp(scores - highest)
    summed = jnp.sum(exponent, axis=-1, keepdims=True)
    attention = (exponent / summed).astype(jnp.bfloat16)
    mixed = jnp.einsum("hqk,khd->qhd", attention, values_all, preferred_element_type=jnp.float32)
    return (mixed.astype(jnp.bfloat16), highest + jnp.log(summed))


def attend_backward(pieces):
    queries, keys_all, values_all, upstream, logsum, length = pieces
    factor = 1.0 / math.sqrt(queries.shape[-1])
    attention = jnp.exp(masked_scores(queries, keys_all, length) - logsum)
    grad_attention = jnp.einsum(
        "qhd,khd->hqk", upstream, values_all, preferred_element_type=jnp.float32
    )
    grad_values = jnp.einsum(
        "hqk,qhd->khd", attention.astype(jnp.bfloat16), upstream, preferred_element_type=jnp.float32
    )
    projected = jnp.sum(attention * grad_attention, axis=-1, keepdims=True)
    grad_scores = (attention * (grad_attention - projected)).astype(jnp.bfloat16)
    grad_queries = (
        jnp.einsum("hqk,khd->qhd", grad_scores, keys_all, preferred_element_type=jnp.float32)
        * factor
    )
    grad_keys = (
        jnp.einsum("hqk,qhd->khd", grad_scores, queries, preferred_element_type=jnp.float32)
        * factor
    )
    return (grad_queries, grad_keys, grad_values)


def local(
    inputs,
    lengths,
    weight_query,
    bias_query,
    weight_key,
    weight_value,
    bias_value,
    weight_out,
    bias_out,
    weight_in,
    bias_in,
    weight_down,
    bias_down,
    first_gain,
    first_shift,
    second_gain,
    second_shift,
    cotangent,
):
    local_width = weight_query.shape[1]
    sequences = lengths.shape[0]
    head_count = local_width // HEAD
    layout = (sequences, SEQ_LEN, head_count, HEAD)
    gathered = lax.all_gather(inputs, "tensor", axis=0, tiled=True)
    all_rows = gathered.shape[0]
    joined = jnp.concatenate([weight_query, weight_key, weight_value], axis=1)
    projected = jnp.dot(gathered, joined, preferred_element_type=jnp.float32)
    queries = (projected[:, :local_width] + bias_query.astype(jnp.float32)).astype(jnp.bfloat16)
    keys_all = projected[:, local_width : 2 * local_width].astype(jnp.bfloat16)
    values_all = (projected[:, 2 * local_width :] + bias_value.astype(jnp.float32)).astype(
        jnp.bfloat16
    )
    query_blocks = queries.reshape(layout)
    key_blocks = keys_all.reshape(layout)
    value_blocks = values_all.reshape(layout)
    mixed, logsum = lax.map(attend_forward, (query_blocks, key_blocks, value_blocks, lengths))
    attended = mixed.reshape(all_rows, local_width)
    branch = lax.psum_scatter(
        jnp.dot(attended, weight_out, preferred_element_type=jnp.float32),
        "tensor",
        scatter_dimension=0,
        tiled=True,
    )
    first_sum = inputs.astype(jnp.float32) + branch + bias_out.astype(jnp.float32)
    normed, first_back = jax.vjp(
        layer_norm, first_sum, first_gain.astype(jnp.float32), first_shift.astype(jnp.float32)
    )
    normed_all = lax.all_gather(normed.astype(jnp.bfloat16), "tensor", axis=0, tiled=True)
    lifted = jnp.dot(normed_all, weight_in, preferred_element_type=jnp.float32) + bias_in.astype(
        jnp.float32
    )
    activated, gelu_back = jax.vjp(gelu_exact, lifted)
    activated_low = activated.astype(jnp.bfloat16)
    feed = lax.psum_scatter(
        jnp.dot(activated_low, weight_down, preferred_element_type=jnp.float32).astype(
            jnp.bfloat16
        ),
        "tensor",
        scatter_dimension=0,
        tiled=True,
    ).astype(jnp.float32)
    second_sum = normed + feed + bias_down.astype(jnp.float32)
    results, second_back = jax.vjp(
        layer_norm, second_sum, second_gain.astype(jnp.float32), second_shift.astype(jnp.float32)
    )
    grad_second, grad_second_gain, grad_second_shift = second_back(cotangent.astype(jnp.float32))
    grad_bias_down = jnp.sum(grad_second, axis=0)
    feed_grads = lax.all_gather(grad_second.astype(jnp.bfloat16), "tensor", axis=0, tiled=True)
    grad_weight_down = contract_rows(activated_low, feed_grads)
    grad_activated = contract_cols(feed_grads, weight_down)
    grad_lifted = gelu_back(grad_activated)[0]
    grad_bias_in = jnp.sum(grad_lifted, axis=0)
    lifted_low = grad_lifted.astype(jnp.bfloat16)
    grad_weight_in = contract_rows(normed_all, lifted_low)
    grad_normed = grad_second + lax.psum_scatter(
        contract_cols(lifted_low, weight_in), "tensor", scatter_dimension=0, tiled=True
    )
    grad_first, grad_first_gain, grad_first_shift = first_back(grad_normed)
    grad_bias_out = jnp.sum(grad_first, axis=0)
    branch_grads = lax.all_gather(grad_first.astype(jnp.bfloat16), "tensor", axis=0, tiled=True)
    grad_weight_out = contract_rows(attended, branch_grads)
    upstream = contract_cols(branch_grads, weight_out).astype(jnp.bfloat16)
    grad_query_blocks, grad_key_blocks, grad_value_blocks = lax.map(
        attend_backward,
        (query_blocks, key_blocks, value_blocks, upstream.reshape(layout), logsum, lengths),
    )
    grad_queries = grad_query_blocks.reshape(all_rows, local_width)
    grad_keys = grad_key_blocks.reshape(all_rows, local_width)
    grad_values = grad_value_blocks.reshape(all_rows, local_width)
    grad_bias_query = jnp.sum(grad_queries, axis=0)
    grad_bias_value = jnp.sum(grad_values, axis=0)
    grad_joined = jnp.concatenate([grad_queries, grad_keys, grad_values], axis=1).astype(
        jnp.bfloat16
    )
    grad_weights_joined = contract_rows(gathered, grad_joined)
    grad_inputs = grad_first + lax.psum_scatter(
        contract_cols(grad_joined, joined).astype(jnp.bfloat16),
        "tensor",
        scatter_dimension=0,
        tiled=True,
    ).astype(jnp.float32)
    (
        grad_bias_out,
        grad_bias_down,
        grad_first_gain,
        grad_first_shift,
        grad_second_gain,
        grad_second_shift,
    ) = lax.psum(
        (
            grad_bias_out,
            grad_bias_down,
            grad_first_gain,
            grad_first_shift,
            grad_second_gain,
            grad_second_shift,
        ),
        ("dp", "tensor"),
    )
    grad_weight_query = grad_weights_joined[:, :local_width]
    grad_weight_key = grad_weights_joined[:, local_width : 2 * local_width]
    grad_weight_value = grad_weights_joined[:, 2 * local_width :]
    (
        grad_weight_query,
        grad_bias_query,
        grad_weight_key,
        grad_weight_value,
        grad_bias_value,
        grad_weight_out,
        grad_weight_in,
        grad_bias_in,
        grad_weight_down,
    ) = lax.psum(
        (
            grad_weight_query,
            grad_bias_query,
            grad_weight_key,
            grad_weight_value,
            grad_bias_value,
            grad_weight_out,
            grad_weight_in,
            grad_bias_in,
            grad_weight_down,
        ),
        "dp",
    )
    return (
        results.astype(jnp.bfloat16),
        grad_inputs,
        grad_weight_query,
        grad_bias_query,
        grad_weight_key,
        grad_weight_value,
        grad_bias_value,
        grad_weight_out,
        grad_bias_out,
        grad_weight_in,
        grad_bias_in,
        grad_weight_down,
        grad_bias_down,
        grad_first_gain,
        grad_first_shift,
        grad_second_gain,
        grad_second_shift,
    )


def solution(mesh):
    in_specs = (
        P(("dp", "tensor"), None),
        P("dp"),
        P(None, "tensor"),
        P("tensor"),
        P(None, "tensor"),
        P(None, "tensor"),
        P("tensor"),
        P("tensor", None),
        P(),
        P(None, "tensor"),
        P("tensor"),
        P("tensor", None),
        P(),
        P(),
        P(),
        P(),
        P(),
        P(("dp", "tensor"), None),
    )
    out_specs = (
        P(("dp", "tensor"), None),
        P(("dp", "tensor"), None),
        P(None, "tensor"),
        P("tensor"),
        P(None, "tensor"),
        P(None, "tensor"),
        P("tensor"),
        P("tensor", None),
        P(),
        P(None, "tensor"),
        P("tensor"),
        P("tensor", None),
        P(),
        P(),
        P(),
        P(),
        P(),
    )
    return jax.shard_map(local, mesh=mesh, in_specs=in_specs, out_specs=out_specs, check_vma=False)
```

profile of v0, /device:TPU:0, one launch (start us, length us, event | category | flops | bytes accessed | tf_op | source)
XLA Modules:
  0.0 731.2 jit_solution(16374877845422942333)
XLA Ops:
  12.3 28.6 %all-gather.5.cloned.1.call-done = bf16[2048,768]{1,0:T(8,128)(2,1)} async-done(((bf16[512,768]{1,0:T(8,128)(2,1)}), bf16[2048,768]{1,0:T(8,128)(2,1)}) %all-gather.5.cloned.1.call-update) | async-done | bytes 3145744 | tf_op jit(solution)/shard_map/all_gather | solution.py:101
  40.9 3.9 convolution_bitcast_fusion
  46.7 3.0 reshape.167
  49.7 1.3 copy.51
  51.0 1.5 reshape.168
  52.4 1.3 copy.52
  53.7 20.0 %while.26 = (s32[]{:T(128)}, bf16[4,512,3,64]{1,3,2,0:T(8,128)(2,1)}, f32[4,3,512,1]{2,1,3,0:T(4,128)}, bf16[4,512,3,64]{1,3,2,0:T(8,128)(2,1)S(1)}, s32[4]{0:T(...) while((s32[]{:T(128)}, ...), condition=%wide.region_3.4_spmd, body=%wide.region_0.3_spmd.sunk | while | flops 210861056 | bytes 10283621 | solution.py:113
  57.1 1.6 fusion.125
  62.1 1.6 fusion.125
  67.1 1.6 fusion.125
  72.0 1.6 fusion.125
  73.7 2.3 copy.53
  77.1 3.7 fusion.77
  81.5 57.8 %reduce-scatter.5.cloned.1.call-done = f32[512,768]{1,0:T(8,128)} async-done(((f32[2048,768]{1,0:T(8,128)}), f32[512,768]{1,0:T(8,128)}) %reduce-scatter.5.cloned.1.call-update) | async-done | bytes 1572880 | tf_op jit(solution)/shard_map/reduce_scatter | solution.py:115
  139.4 1.9 fusion.73
  142.2 1.2 fusion.65
  144.0 1.3 convert_element_type.98
  145.2 26.8 %all-gather.7.cloned.1.call-done = bf16[2048,768]{1,0:T(8,128)(2,1)} async-done(((bf16[512,768]{1,0:T(8,128)(2,1)}), bf16[2048,768]{1,0:T(8,128)(2,1)}) %all-gather.7.cloned.1.call-update) | async-done | bytes 3145744 | tf_op jit(solution)/shard_map/all_gather | solution.py:125
  172.1 18.4 %multiply_convert_fusion.1 = (bf16[2048,768]{1,0:T(8,128)(2,1)S(1)}, f32[2048,768]{1,0:T(8,128)}, f32[2048,768]{1,0:T(8,128)}) fusion(f32[768]{0:T(1024)} %convert_element_type.98, bf16[2048,768]{1,0:T(8,128)(2,1)} %all-gather.7.cloned.1.call-done, bf16[768,768]{1,0:T(8,128)(2,1)S(1)} %copy-done), kind=kOutput, calls=%fused_computation.60 | convolution fusion | flops 2519728128 | bytes 20057088 | tf_op jit(solution)/shard_map/dot_general | solution.py:126
  190.5 1.7 copy-done.42
  192.1 4.0 convolution_convert_fusion
  196.2 1.3 convert_element_type.102
  197.5 1.3 convert_element_type.103
  198.8 1.3 convert_element_type.104
  200.0 34.2 %reduce-scatter.7.cloned.1.call-done = bf16[512,768]{1,0:T(8,128)(2,1)} async-done(((bf16[2048,768]{1,0:T(8,128)(2,1)}), bf16[512,768]{1,0:T(8,128)(2,1)}) %reduce-scatter.7.cloned.1.call-update) | async-done | bytes 786448 | tf_op jit(solution)/shard_map/reduce_scatter | solution.py:131
  234.3 1.8 fusion.71
  236.4 1.2 fusion.58
  237.7 1.6 fusion.70
  240.4 1.7 add_reduce_fusion.1
  242.3 28.5 %all-gather.9.cloned.1.call-done = bf16[2048,768]{1,0:T(8,128)(2,1)} async-done(((bf16[512,768]{1,0:T(8,128)(2,1)}), bf16[2048,768]{1,0:T(8,128)(2,1)}) %all-gather.9.cloned.1.call-update) | async-done | bytes 3145744 | tf_op jit(solution)/shard_map/all_gather | solution.py:145
  270.8 11.0 %fusion.68 = (f32[768]{0:T(1024)}, bf16[2048,768]{1,0:T(8,128)(2,1)S(1)}) fusion(f32[2048,768]{1,0:T(8,128)} %get-tuple-element.213, f32[2048,768]{1,0:T(8,128)} %get-tuple-element.234, f32[768]{0:T(1024)} %convert_element_type.98, bf16[2048,768]{1,0:T(8,128)(2,1)} %all-gather.9.cloned.1.call-done, bf16[768,768]{1,0:T(8,128)(2,1)} %param.33), kind=kOutput, calls=%fused_computation.128 | convolution fusion | flops 2441084160 | bytes 20060160 | tf_op jit(solution)/shard_map/dot_general | solution.py:29
  281.8 1.7 copy-done.43
  283.5 4.5 fusion.63
  288.1 58.5 %reduce-scatter.9.cloned.1.call-done = f32[512,768]{1,0:T(8,128)} async-done(((f32[2048,768]{1,0:T(8,128)}), f32[512,768]{1,0:T(8,128)}) %reduce-scatter.9.cloned.1.call-update) | async-done | bytes 1572880 | tf_op jit(solution)/shard_map/reduce_scatter | solution.py:152
  346.6 3.3 multiply_reduce_fusion.1
  350.6 1.2 copy-done.4
  353.1 28.4 %all-gather.11.cloned.1.call-done = bf16[2048,768]{1,0:T(8,128)(2,1)} async-done(((bf16[512,768]{1,0:T(8,128)(2,1)}), bf16[2048,768]{1,0:T(8,128)(2,1)}) %all-gather.11.cloned.1.call-update) | async-done | bytes 3145744 | tf_op jit(solution)/shard_map/all_gather | solution.py:157
  381.5 3.1 convolution_convert_fusion.2
  385.7 34.3 %while.27 = (s32[]{:T(128)}, f32[4,512,3,64]{1,3,2,0:T(8,128)}, bf16[4,512,3,64]{1,3,2,0:T(8,128)(2,1)}, f32[4,512,3,64]{1,3,2,0:T(8,128)}, bf16[4,512,3,64]{1,3...) while((s32[]{:T(128)}, f32[4,512,3,64]{1,3,2,0:T(8,128)}, ...), condition=%wide.region_17.18_spmd, body=%wide.region_15.17_spmd.sunk | while | flops 510589952 | bytes 32479416 | solution.py:160
  385.7 1.5 fusion.134
  393.0 1.4 fusion.137
  394.3 1.5 fusion.134
  401.5 1.4 fusion.137
  402.9 1.5 fusion.134
  410.1 1.4 fusion.137
  411.5 1.5 fusion.134
  418.7 1.4 fusion.137
  420.1 3.4 fusion.75
  426.3 1.4 copy-done.20
  427.7 4.0 convolution_convert_fusion.1
  432.1 7.1 fusion.79
  439.3 4.1 fusion.61
  443.4 2.0 convolution_bitcast_fusion.1
  445.4 1.2 fusion.74
  446.9 1.6 fusion.78
  449.3 40.4 %all-reduce = (f32[768]{0:T(1024)}, f32[768]{0:T(1024)}, f32[768]{0:T(1024)}, f32[768]{0:T(1024)}, f32[768]{0:T(1024)}, /*index=5*/f32[768]{0:T(1024)}) all-reduce(f32[768]{0:T(1024)S(1)} %get-tuple-element.228, f32[768]{0:T(1024)S(1)} %copy-done.30, f32[768]{0:T(1024)S(1)} %copy-done.31, ...), channel_id=1, replica_groups=mesh['dp'=8,'tensor'=4] {'dp','tensor'}, use_global_device_ids=true, to_apply=%region_28.29 | all-reduce | flops 4608 | bytes 36864 | tf_op jit(solution)/shard_map/psum | solution.py:186
  489.9 23.7 %all-reduce.1 = (f32[192]{0:T(256)}, f32[192]{0:T(256)}, f32[768]{0:T(1024)}) all-reduce(f32[192]{0:T(256)S(1)} %reduce_sum.216, f32[192]{0:T(256)S(1)} %reduce_sum.218, f32[768]{0:T(1024)S(1)} %copy-done.33), channel_id=1, replica_groups=mesh['dp'=8,'tensor'=4] {'dp'}, use_global_device_ids=true, to_apply=%region_21.22 | all-reduce | flops 1152 | bytes 9216 | tf_op jit(solution)/shard_map/psum | solution.py:210
  513.6 2.5 convert_add_fusion
  516.1 198.8 %all-reduce.5.cloned.1.call-done = (f32[768,192]{0,1:T(8,128)}, f32[768,192]{0,1:T(8,128)}, f32[768,192]{0,1:T(8,128)}, f32[192,768]{1,0:T(8,128)}, f32[768,768]{1,0:T(8,128)}, /*index=5*/f32[768,768]{1,0:T(8,128)}) async-done(((f32[768,192]{0,1:T(8,128)}, f32[768,192]{0,1:T(8,128)}, f32[768,192]{0,1:T(8,128)}, f32[192,768]{1,0:T(8,128)}, f32[768,768]{1,0:T(8,128)}, /*index=5*/f32[768,768]{1,0:T(8,128)}), ...) | async-done | bytes 7077904 | tf_op jit(solution)/shard_map/psum | solution.py:210
  714.9 2.1 copy.107
  716.9 1.9 copy.108
  718.9 1.9 copy.109
  721.6 1.4 copy.111
  723.0 1.4 copy.112
  (209 shorter events, 56.2 us)
Async XLA Ops:
  7.2 164.9 %copy-start = (bf16[768,768]{1,0:T(8,128)(2,1)S(1)}, bf16[768,768]{1,0:T(8,128)(2,1)}, u32[]{:S(2)}) copy-start(bf16[768,768]{1,0:T(8,128)(2,1)} %param.31) | copy-start | bytes 3538948
  7.2 33.7 %all-gather.5.cloned.1.call-start = ((), (), s32[]{:S(2)}) async-start(), calls=%async_computation.4 | async-start | bytes 3932160 | tf_op jit(solution)/shard_map/all_gather | solution.py:101
  7.9 131.4 %reduce-scatter.5.cloned.1.call-start = ((), (), s32[]{:S(2)}) async-start(), calls=%async_computation.5 | async-start | bytes 7864320 | tf_op jit(solution)/shard_map/reduce_scatter | solution.py:115
  12.3 28.6 %copy-start.22 = (bf16[768,576]{0,1:T(8,128)(2,1)}, bf16[768,576]{0,1:T(8,128)(2,1)S(1)}, u32[]{:S(2)}) copy-start(bf16[768,576]{0,1:T(8,128)(2,1)S(1)} %constant_dynamic-update-slice_fusion) | copy-start | bytes 2654212
  46.7 7.0 copy-start.40
  73.7 7.1 copy-start.2
  73.7 7.1 copy-start.9
  73.7 3.4 copy-start.18
  76.2 0.9 copy-start.7
  80.8 0.7 copy-start.34
  80.8 0.7 copy-start.35
  80.8 0.7 copy-start.36
  80.9 91.2 %all-gather.7.cloned.1.call-start = ((), (), s32[]{:S(2)}) async-start(), calls=%async_computation.6 | async-start | bytes 3932160 | tf_op jit(solution)/shard_map/all_gather | solution.py:125
  141.6 0.6 copy-start.25
  143.4 90.9 %reduce-scatter.7.cloned.1.call-start = ((), (), s32[]{:S(2)}) async-start(), calls=%async_computation.7 | async-start | bytes 3932160 | tf_op jit(solution)/shard_map/reduce_scatter | solution.py:131
  172.1 20.1 %copy-start.39 = (bf16[768,768]{1,0:T(8,128)(2,1)S(1)}, bf16[768,768]{1,0:T(8,128)(2,1)}, u32[]{:S(2)}) copy-start(bf16[768,768]{1,0:T(8,128)(2,1)} %param.33) | copy-start | bytes 3538948
  190.5 1.7 copy-start.42
  196.2 74.6 %all-gather.9.cloned.1.call-start = ((), (), s32[]{:S(2)}) async-start(), calls=%async_computation.8 | async-start | bytes 3932160 | tf_op jit(solution)/shard_map/all_gather | solution.py:145
  234.3 2.2 copy-start.11
  234.3 2.2 copy-start.24
  234.3 3.4 copy-start.27
  239.3 1.1 copy-start.6
  242.1 104.5 %reduce-scatter.9.cloned.1.call-start = ((), (), s32[]{:S(2)}) async-start(), calls=%async_computation.9 | async-start | bytes 7864320 | tf_op jit(solution)/shard_map/reduce_scatter | solution.py:152
  281.8 1.7 copy-start.43
  288.1 61.8 %copy-start.26 = (f32[512]{0:T(512)S(1)}, f32[512]{0:T(512)}, u32[]{:S(2)}) copy-start(f32[512]{0:T(512)} %copy-done.25) | copy-start | bytes 6148
  288.1 93.5 %all-gather.11.cloned.1.call-start = ((), (), s32[]{:S(2)}) async-start(), calls=%async_computation.10 | async-start | bytes 3932160 | tf_op jit(solution)/shard_map/all_gather | solution.py:157
  349.9 31.6 %copy-start.19 = (bf16[192,768]{1,0:T(8,128)(2,1)S(1)}, bf16[192,768]{1,0:T(8,128)(2,1)}, u32[]{:S(2)}) copy-start(bf16[192,768]{1,0:T(8,128)(2,1)} %param.29) | copy-start | bytes 884740
  350.5 1.2 copy-start.4
  352.9 160.8 %reduce-scatter.11.cloned.1.call-start = ((), (), s32[]{:S(2)}) async-start(), calls=%async_computation.11 | async-start | bytes 3932160 | tf_op jit(solution)/shard_map/reduce_scatter | solution.py:173
  384.6 1.1 copy-start.3
  384.6 1.1 copy-start.41
  390.4 2.0 copy-start.14
  393.0 1.4 copy-start.15
  398.9 2.0 copy-start.14
  401.5 1.4 copy-start.15
  407.5 2.0 copy-start.14
  410.1 1.4 copy-start.15
  416.1 2.0 copy-start.14
  418.7 1.4 copy-start.15
  423.5 1.1 copy-start.16
  425.4 2.3 copy-start.23
  426.3 1.4 copy-start.20
  431.8 283.1 %all-reduce.5.cloned.1.call-start = ((), (), s32[]{:S(2)}) async-start(), calls=%async_computation.12 | async-start | bytes 14155776 | tf_op jit(solution)/shard_map/psum | solution.py:210
  432.1 7.1 copy-start.38
  432.1 7.1 copy-start.44
  439.2 4.1 copy-start.21
  439.2 4.1 copy-start.37
  443.4 3.3 copy-start.10
  445.4 1.6 copy-start.8
  448.6 0.7 copy-start.28
  448.6 0.7 copy-start.29
  448.6 0.7 copy-start.30
  448.6 0.7 copy-start.31
  448.6 0.7 copy-start.32
  448.6 41.3 %copy-start.33 = (f32[768]{0:T(1024)S(1)}, f32[768]{0:T(1024)}, u32[]{:S(2)}) copy-start(f32[768]{0:T(1024)} %get-tuple-element.203) | copy-start | bytes 9220
  448.6 65.0 %copy-start.5 = (f32[512,768]{1,0:T(8,128)S(1)}, f32[512,768]{1,0:T(8,128)}, u32[]{:S(2)}) copy-start(f32[512,768]{1,0:T(8,128)} %copy-done.4) | copy-start | bytes 4718596
  714.9 5.9 copy-start.17
  714.9 6.7 copy-start.13
  720.8 2.2 copy-start.12
  721.6 2.8 copy-start.1
Sparse Core Ops, SparseCore 0:
  9.6 31.2 all-gather.4
  81.0 58.3 reduce-scatter.4
  143.5 28.5 all-gather.6
  196.3 37.9 reduce-scatter.6
  242.2 28.5 all-gather.8
  288.2 58.3 reduce-scatter.8
  353.0 28.5 all-gather.10
  431.9 38.6 reduce-scatter.10
  476.8 238.0 all-reduce.4
where the time goes:
time: 740 us; the launch traced here: 731 us
  waiting for transfers between devices  462 us (62%)
  matrix products  100 us (14%)
  blocking collectives  64.1 us (9%)
  local copies, waits for them, and re-layouts  45.9 us (6%)
  other arithmetic  42.3 us (6%)
  between operations  14.6 us (2%)
    psum x1, waiting for transfers between devices, local(): lax.psum((grad_weight_query, grad_bias_query, grad_weight_key, grad_weigh...  199 us
    reduce_scatter x1, waiting for transfers between devices, local(): lax.psum_scatter(contract_cols(lifted_low, weight_in), 'tensor', scatter_...  58.5 us
    reduce_scatter x1, waiting for transfers between devices, local(): lax.psum_scatter(jnp.dot(attended, weight_out, preferred_element_type=jnp...  57.8 us
    psum x1, blocking collectives, local(): lax.psum((grad_bias_out, grad_bias_down, grad_first_gain, grad_first_shif...  40.4 us
    reduce_scatter x1, waiting for transfers between devices, local(): lax.psum_scatter(jnp.dot(activated_low, weight_down, preferred_element_ty...  34.2 us
    all_gather x1, waiting for transfers between devices, local(): gathered = lax.all_gather(inputs, 'tensor', axis=0, tiled=True)  28.6 us
    all_gather x1, waiting for transfers between devices, local(): lax.all_gather(grad_second.astype(jnp.bfloat16), 'tensor', axis=0, tiled=...  28.5 us
    all_gather x1, waiting for transfers between devices, local(): lax.all_gather(grad_first.astype(jnp.bfloat16), 'tensor', axis=0, tiled=T...  28.4 us
  transfers between devices with their start and end apart: 9, of which 8 were waited for; matrix products, arithmetic and copies ran while one was open for 4% of the time, Pallas kernels for 0%

commit v1 on v0

v1 whole, which is shorter than its diff:
```python
import functools
import math

import jax
import jax.numpy as jnp
from jax import lax
from jax.experimental import pallas as pl
from jax.experimental.pallas import tpu as pltpu
from jax.sharding import PartitionSpec as P

HEAD = 64
SEQ_LEN = 512
UP_ROWS = 128
F32 = jnp.float32
BF16 = jnp.bfloat16
VMEM_LIMIT = 24 * 1024 * 1024
VMEM = pl.BlockSpec(memory_space=pltpu.VMEM)
COST = pl.CostEstimate(flops=10**9, bytes_accessed=10**9, transcendentals=0)
MIDDLE = pl.CostEstimate(flops=10**10, bytes_accessed=10**9, transcendentals=0)
LONG = pl.CostEstimate(flops=10**11, bytes_accessed=10**9, transcendentals=0)
SMEM = pl.BlockSpec(memory_space=pltpu.SMEM)
HBM = pl.BlockSpec(memory_space=pltpu.HBM)


def hbm(shape, dtype=BF16):
    return pltpu.HBM(shape, dtype)


def pinned(value):
    return pltpu.with_memory_space_constraint(value, pltpu.HBM)


def dot(left, right, left_dim, right_dim):
    return lax.dot_general(
        left, right, (((left_dim,), (right_dim,)), ((), ())), preferred_element_type=F32
    )


def params(**kwargs):
    return pltpu.CompilerParams(vmem_limit_bytes=VMEM_LIMIT, **kwargs)


def whole(shape, index=None):
    place = index or (0,) * len(shape)
    return pl.BlockSpec(shape, lambda *_: place)


def row(ref):
    return ref[...].astype(F32).reshape(1, ref.shape[0])


def pack_rows(width):
    return (4 * width + 16 + 63) // 64 * 64


def bit(spot_ref, number):
    return lax.rem(lax.div(spot_ref[0], 2**number), 2)


def window(choice, size, tile):
    return pl.ds(pl.multiple_of(choice * size, tile), size)


def quarter(spot_ref, r, size):
    first = lax.rem(bit(spot_ref, 0) + r // 2, 2)
    second = lax.rem(bit(spot_ref, 1) + r % 2, 2)
    return window(2 * first + second, size, 16)


def run(copies):
    for one in copies:
        one.start()
    for one in copies:
        one.wait()


def prepare_pack_kernel(spot_ref, q_ref, k_ref, v_ref, out_ref, bq_ref, bv_ref, bin_ref, *refs):
    full_ref, first_ref, last_ref, held_ref, extra_ref, bq, bv, bin_, sems = refs
    width = out_ref.shape[0]
    copies = [
        pltpu.make_async_copy(ref, held_ref.at[pl.ds(i * width, width), :], sems.at[i])
        for i, ref in enumerate((q_ref, k_ref, v_ref, out_ref))
    ]
    vectors = [
        pltpu.make_async_copy(ref, to, sems.at[4 + i])
        for i, (ref, to) in enumerate(((bq_ref, bq), (bv_ref, bv), (bin_ref, bin_)))
    ]
    for one in vectors + copies:
        one.start()
    extra_ref[...] = jnp.zeros_like(extra_ref)
    for one in vectors:
        one.wait()
    extra_ref[0, :width] = bq[...].astype(F32)
    extra_ref[0, 2 * width : 3 * width] = bv[...].astype(F32)
    extra_ref[1, :] = bin_[...].astype(F32)
    held_ref[4 * width :, :] = extra_ref[...].astype(BF16)
    for one in copies:
        one.wait()
    size = first_ref.shape[0]
    run(
        [
            pltpu.make_async_copy(held_ref.at[quarter(spot_ref, 0, size), :], first_ref, sems.at[0]),
            pltpu.make_async_copy(held_ref.at[quarter(spot_ref, 3, size), :], last_ref, sems.at[1]),
            pltpu.make_async_copy(held_ref, full_ref, sems.at[2]),
        ]
    )


def prepare_pack(spot, wq, wk, wv, wout, bq, bv, bin_):
    width, model = wout.shape
    rows = pack_rows(width)
    return pl.pallas_call(
        prepare_pack_kernel,
        out_shape=(hbm((rows, model)), hbm((rows // 4, model)), hbm((rows // 4, model))),
        in_specs=[SMEM] + [HBM] * 7,
        out_specs=(HBM,) * 3,
        scratch_shapes=[
            pltpu.VMEM((rows, model), BF16),
            pltpu.VMEM((rows - 4 * width, model), F32),
            pltpu.VMEM(bq.shape, BF16),
            pltpu.VMEM(bv.shape, BF16),
            pltpu.VMEM(bin_.shape, BF16),
            pltpu.SemaphoreType.DMA((7,)),
        ],
        compiler_params=params(),
        name="prepare_pack",
    )(spot, *(pinned(one) for one in (wq.T, wk.T, wv.T, wout, bq, bv, bin_)))


def prepare_feed_kernel(spot_ref, win_ref, wd_ref, *refs):
    outs, held, sems = refs[:4], refs[4:8], refs[8]
    size = outs[0].shape[0]
    loads = []
    for i in range(4):
        source = (win_ref, wd_ref)[i // 2].at[quarter(spot_ref, 3 * (i % 2), size), :]
        loads.append(pltpu.make_async_copy(source, held[i], sems.at[i]))
        loads[i].start()
    stores = []
    for i in range(4):
        loads[i].wait()
        stores.append(pltpu.make_async_copy(held[i], outs[i], sems.at[i]))
        stores[i].start()
    for one in stores:
        one.wait()


def prepare_feed(spot, win, wd):
    size, model = win.shape[0] // 4, win.shape[1]
    return pl.pallas_call(
        prepare_feed_kernel,
        out_shape=(hbm((size, model)),) * 4,
        in_specs=[SMEM, HBM, HBM],
        out_specs=(HBM,) * 4,
        scratch_shapes=[pltpu.VMEM((size, model), BF16)] * 4 + [pltpu.SemaphoreType.DMA((4,))],
        compiler_params=params(),
        name="prepare_feed",
    )(spot, pinned(win), pinned(wd))


def finish_pack_kernel(spot_ref, *refs):
    parts, (q_ref, k_ref, v_ref, out_ref, extra_ref, held_ref) = refs[:4], refs[4:]
    size = parts[0].shape[0]
    width = q_ref.shape[0]
    for r in range(4):
        held_ref[quarter(spot_ref, r, size), :] = parts[r][...]
    for i, ref in enumerate((q_ref, k_ref, v_ref, out_ref)):
        ref[...] = held_ref[i * width : (i + 1) * width, :].astype(F32)
    extra_ref[...] = held_ref[4 * width : 4 * width + 16, :].astype(F32)


def finish_pack(spot, parts, width):
    size, model = parts[0].shape
    one = jax.ShapeDtypeStruct((width, model), F32)
    return pl.pallas_call(
        finish_pack_kernel,
        out_shape=(one,) * 4 + (jax.ShapeDtypeStruct((16, model), F32),),
        in_specs=[SMEM] + [VMEM] * 4,
        out_specs=(VMEM,) * 5,
        scratch_shapes=[pltpu.VMEM((4 * size, model), BF16)],
        compiler_params=params(),
        cost_estimate=COST,
        name="finish_pack",
    )(spot, *parts)


def finish_block_kernel(spot_ref, *refs):
    for r in range(4):
        refs[4][quarter(spot_ref, r, refs[r].shape[0]), :] = refs[r][...].astype(F32)


def finish_block(spot, parts):
    size, model = parts[0].shape
    return pl.pallas_call(
        finish_block_kernel,
        out_shape=jax.ShapeDtypeStruct((4 * size, model), F32),
        in_specs=[SMEM] + [VMEM] * 4,
        out_specs=VMEM,
        compiler_params=params(),
        cost_estimate=COST,
        name="finish_block",
    )(spot, *parts)


def attend_forward_kernel(pieces, length_ref, seq_ref, spot_ref, x_ref, *refs):
    parts, refs = refs[:pieces], refs[pieces:]
    if pieces > 1:
        pack_out, *refs, pack_ref = refs
    else:
        pack_ref = parts[0]
    qkv_out, e_out, r_out, att_out, bias_out, qkv_ref, e_ref, r_ref, att_ref, sems = refs
    width = att_ref.shape[0]
    heads = width // HEAD
    if pieces == 1:
        bias_out[...] = pack_ref[4 * width : 4 * width + 16, :]
    scale = math.log2(math.e) / math.sqrt(HEAD)
    copies = []

    def store(source, target, sem):
        copies.append(pltpu.make_async_copy(source, target, sems.at[sem]))
        copies[-1].start()

    if pieces > 1:
        size = parts[0].shape[0]
        for r in range(4):
            pack_ref[quarter(spot_ref, r, size), :] = parts[r][...]
        store(pack_ref, pack_out, heads)
        bias_out[...] = pack_ref[4 * width : 4 * width + 16, :]
    bias = jnp.transpose(pack_ref[4 * width : 4 * width + 16, :].astype(F32))[: 3 * width, 0:1]
    projected = dot(pack_ref[: 3 * width, :], x_ref[...], 1, 1) + bias
    qkv_ref[...] = projected.astype(BF16)
    store(qkv_ref, qkv_out, heads + 1)
    visible = lax.broadcasted_iota(jnp.int32, (SEQ_LEN, 1), 0) < length_ref[seq_ref[0]]
    for h in range(heads):
        rows = slice(h * HEAD, (h + 1) * HEAD)
        q = qkv_ref[h * HEAD : (h + 1) * HEAD, :]
        k = qkv_ref[width + h * HEAD : width + (h + 1) * HEAD, :]
        v = qkv_ref[2 * width + h * HEAD : 2 * width + (h + 1) * HEAD, :]
        scores = jnp.where(visible, dot(k, q, 0, 0) * scale, -1e30)
        highest = jnp.max(scores, axis=0, keepdims=True)
        e = jnp.exp2(scores - highest)
        r = 1.0 / jnp.sum(e, axis=0, keepdims=True)
        low = e.astype(BF16)
        e_ref[h] = low
        store(e_ref.at[h], e_out.at[h], h)
        r_ref[h : h + 1, :] = r
        att_ref[rows, :] = (dot(v, low, 1, 0) * r).astype(BF16)
    store(r_ref, r_out, heads + 2)
    store(att_ref, att_out, heads + 3)
    for one in copies:
        one.wait()


def attend_forward(scalars, x, parts):
    rows, model = x.shape
    width = model // 4
    heads = width // HEAD
    pieces = len(parts)
    full = hbm((pieces * parts[0].shape[0], model))
    held = [hbm((3 * width, rows)), hbm((heads, rows, rows)), hbm((8, rows), F32), hbm((width, rows))]
    more = [full] if pieces > 1 else []
    outs = pl.pallas_call(
        functools.partial(attend_forward_kernel, pieces),
        out_shape=(*more, *held, jax.ShapeDtypeStruct((16, model), BF16)),
        in_specs=[SMEM] * 3 + [VMEM] * (1 + pieces),
        out_specs=(HBM,) * (len(more) + 4) + (VMEM,),
        scratch_shapes=[pltpu.VMEM(one.shape, one.dtype) for one in held]
        + [pltpu.SemaphoreType.DMA((heads + 4,))]
        + [pltpu.VMEM(one.shape, one.dtype) for one in more],
        compiler_params=params(),
        cost_estimate=MIDDLE,
        name="attend_forward",
    )(*scalars, x, *parts)
    return outs if more else (parts[0], *outs)


def attend_backward_kernel(count, plus, split, first, spot_ref, x_ref, bg_ref, *refs):
    dbs, (first_ref, second_ref), refs = refs[:count], refs[count : count + 2], refs[count + 2 :]
    saved, refs = refs[: 5 * count], refs[5 * count :]
    add_in, refs = refs[:plus], refs[plus:]
    outs, refs = refs[: 1 + split], refs[1 + split :]
    g_outs, refs = refs[:count], refs[count:]
    held, (extra_ref, sems) = refs[: 7 * count], refs[7 * count : 7 * count + 2]
    factor = 1.0 / math.sqrt(HEAD)

    def move(source, target, *sem):
        copy = pltpu.make_async_copy(source, target, sems.at[sem])
        copy.start()
        return copy

    loads = []
    for n in range(count):
        pack_in, qkv_in, e_in, r_in, att_in = saved[5 * n : 5 * n + 5]
        qkv_ref, e_ref, r_ref, att_ref, wout_ref = held[7 * n : 7 * n + 5]
        width = att_ref.shape[0]
        heads = width // HEAD
        one = [
            move(pack_in.at[pl.ds(3 * width, width), :], wout_ref, n, 0),
            move(qkv_in, qkv_ref, n, 1),
            move(r_in, r_ref, n, 2),
            move(att_in, att_ref, n, 3),
        ]
        loads.append(one + [move(e_in.at[h], e_ref.at[h], n, 4 + h) for h in range(heads)])
    stores = []
    for n in range(count):
        qkv_ref, e_ref, r_ref, att_ref, wout_ref, g_ref, held_ref = held[7 * n : 7 * n + 7]
        size = held_ref.shape[0] // 4
        extra_ref[...] = jnp.zeros_like(extra_ref)
        extra_ref[1:2, :] = dbs[n][0:1, :]
        extra_ref[2:5, :] = first_ref[0:3, :]
        extra_ref[5:8, :] = second_ref[0:3, :]
        loads[n][0].wait()
        up = dot(wout_ref[...], bg_ref[...], 1, 1).astype(BF16).astype(F32)
        for one in loads[n][1:4]:
            one.wait()
        for h in range(heads):
            rows = slice(h * HEAD, (h + 1) * HEAD)
            q = qkv_ref[h * HEAD : (h + 1) * HEAD, :]
            k = qkv_ref[width + h * HEAD : width + (h + 1) * HEAD, :]
            v = qkv_ref[2 * width + h * HEAD : 2 * width + (h + 1) * HEAD, :]
            scaled = up[rows, :] * r_ref[h : h + 1, :]
            inner = jnp.sum(att_ref[rows, :].astype(F32) * scaled, axis=0, keepdims=True)
            do = scaled.astype(BF16)
            loads[n][4 + h].wait()
            e = e_ref[h]
            ds = (e.astype(F32) * (dot(v, do, 0, 0) - inner)).astype(BF16)
            g_ref[h * HEAD : (h + 1) * HEAD, :] = (dot(k, ds, 1, 0) * factor).astype(BF16)
            g_ref[width + h * HEAD : width + (h + 1) * HEAD, :] = (
                dot(q, ds, 1, 1) * factor
            ).astype(BF16)
            g_ref[2 * width + h * HEAD : 2 * width + (h + 1) * HEAD, :] = dot(do, e, 1, 1).astype(
                BF16
            )
        stores.append(move(g_ref, g_outs[n], n, 0))
        g = g_ref[...]
        extra_ref[0:1, : 3 * width] = dot(jnp.ones((8, g.shape[1]), BF16), g, 1, 1)[0:1, :]
        held_ref[4 * width :, :] = extra_ref[...].astype(BF16)
        held_ref[: 3 * width, :] = dot(g, x_ref[...], 1, 0).astype(BF16)
        held_ref[3 * width : 4 * width, :] = dot(att_ref[...], bg_ref[...], 1, 0).astype(BF16)
        for r in range(4):
            if plus:
                part = quarter(spot_ref, r, size)
                value = held_ref[part, :].astype(F32) + add_in[0][first + r].astype(F32)
                held_ref[part, :] = value.astype(BF16)
            if len(outs) == 1:
                target = outs[0].at[4 * n + r]
            else:
                target = outs[1].at[(0, 2, 0, 1)[r]] if r else outs[0]
            stores.append(
                move(held_ref.at[quarter(spot_ref, r, size), :], target, n, 4 + heads + r)
            )
    for one in stores:
        one.wait()


def attend_backward(spot, x, bg, dbs, first, second, saved, split=False, adds=()):
    rows, model = x.shape
    width = model // 4
    heads = width // HEAD
    count = len(dbs)
    full = saved[0][0].shape[0]
    more = list(adds)
    if split:
        grads = (hbm((full // 4, model)), hbm((3, full // 4, model)))
    else:
        grads = (hbm((4 * count, full // 4, model)),)
    flat = [pinned(one) for block in saved for one in block]
    return pl.pallas_call(
        functools.partial(attend_backward_kernel, count, len(more), split, 0 if split else 4),
        out_shape=grads + (hbm((3 * width, rows)),) * count,
        in_specs=[SMEM] + [VMEM] * (4 + count) + [HBM] * (5 * count) + [VMEM] * len(more),
        out_specs=(HBM,) * (len(grads) + count),
        scratch_shapes=[
            pltpu.VMEM((3 * width, rows), BF16),
            pltpu.VMEM((heads, rows, rows), BF16),
            pltpu.VMEM((8, rows), F32),
            pltpu.VMEM((width, rows), BF16),
            pltpu.VMEM((width, model), BF16),
            pltpu.VMEM((3 * width, rows), BF16),
            pltpu.VMEM((full, model), BF16),
        ]
        * count
        + [
            pltpu.VMEM((full - 4 * width, model), F32),
            pltpu.SemaphoreType.DMA((count, 8 + heads)),
        ],
        compiler_params=params(),
        cost_estimate=MIDDLE,
        name="attend_backward",
    )(spot, x, bg, *dbs, first, second, *flat, *more)


def input_grad_kernel(count, acc_ref, *refs):
    gs, packs, out_ref, sems = refs[:count], refs[count : 2 * count], refs[2 * count], refs[-1]
    held_g, held_w = refs[2 * count + 1 : 3 * count + 1], refs[3 * count + 1 : 4 * count + 1]
    width = held_w[0].shape[0]
    loads = []
    for i in range(count):
        loads.append(pltpu.make_async_copy(gs[i], held_g[i], sems.at[2 * i]))
        loads.append(
            pltpu.make_async_copy(packs[i].at[pl.ds(0, width), :], held_w[i], sems.at[2 * i + 1])
        )
    for one in loads:
        one.start()
    total = acc_ref[...]
    for i in range(count):
        loads[2 * i].wait()
        loads[2 * i + 1].wait()
        total = total + dot(held_g[i][...], held_w[i][...], 0, 0)
    out_ref[...] = total


def input_grad(acc, gs, packs):
    rows, model = acc.shape
    width, count = gs[0].shape[0], len(gs)
    return pl.pallas_call(
        functools.partial(input_grad_kernel, count),
        out_shape=jax.ShapeDtypeStruct((rows, model), F32),
        in_specs=[VMEM] + [HBM] * (2 * count),
        out_specs=VMEM,
        scratch_shapes=[pltpu.VMEM((width, rows), BF16)] * count
        + [pltpu.VMEM((width, model), BF16)] * count
        + [pltpu.SemaphoreType.DMA((2 * count,))],
        compiler_params=params(),
        cost_estimate=COST,
        name="input_grad",
    )(acc, *(pinned(one) for one in gs), *(pinned(one) for one in packs))


def first_norm_kernel(x_ref, bias_ref, gain_ref, shift_ref, *refs):
    atts, packs, refs = refs[:4], refs[4:8], refs[8:]
    z_ref, low_ref, turned_ref, rstd_ref = refs[:4]
    held_a, held_w, sems = refs[4], refs[5], refs[6]
    width = atts[0].shape[0]
    loads = []
    for i in range(4):
        part = pl.ds(i * width, width)
        loads.append(pltpu.make_async_copy(atts[i], held_a.at[part, :], sems.at[2 * i]))
        loads.append(
            pltpu.make_async_copy(
                packs[i].at[pl.ds(3 * width, width), :], held_w.at[part, :], sems.at[2 * i + 1]
            )
        )
    run(loads)
    branch = dot(held_a[...], held_w[...], 0, 0)
    total = x_ref[...].astype(F32) + branch + row(bias_ref)
    center = total - jnp.mean(total, axis=1, keepdims=True)
    rstd = lax.rsqrt(jnp.mean(center * center, axis=1, keepdims=True) + 1e-12)
    z = center * rstd
    z_ref[...] = z
    rstd_ref[...] = rstd
    normed = (z * row(gain_ref) + row(shift_ref)).astype(BF16)
    low_ref[...] = normed
    turned_ref[...] = jnp.transpose(normed)


def first_norm(x, vectors, atts, packs):
    rows, model = x.shape
    return pl.pallas_call(
        first_norm_kernel,
        out_shape=(
            jax.ShapeDtypeStruct((rows, model), F32),
            jax.ShapeDtypeStruct((rows, model), BF16),
            jax.ShapeDtypeStruct((model, rows), BF16),
            jax.ShapeDtypeStruct((rows, 1), F32),
        ),
        in_specs=[VMEM] * 4 + [HBM] * 8,
        out_specs=(VMEM,) * 4,
        scratch_shapes=[
            pltpu.VMEM((model, rows), BF16),
            pltpu.VMEM((model, model), BF16),
            pltpu.SemaphoreType.DMA((8,)),
        ],
        compiler_params=params(),
        cost_estimate=MIDDLE,
        name="first_norm",
    )(x, *vectors, *(pinned(one) for one in atts), *(pinned(one) for one in packs))


def second_norm_kernel(z_ref, feed_ref, c_ref, *refs):
    gain1, shift1, bias, gain2, shift2 = (row(ref) for ref in refs[:5])
    out_ref, grad_ref, low_ref, sum_ref = refs[5:]
    total = z_ref[...] * gain1 + shift1 + feed_ref[...] + bias
    center = total - jnp.mean(total, axis=1, keepdims=True)
    rstd = lax.rsqrt(jnp.mean(center * center, axis=1, keepdims=True) + 1e-12)
    z = center * rstd
    out_ref[...] = (z * gain2 + shift2).astype(BF16)
    c = c_ref[...].astype(F32)
    e = c * gain2
    grad = (
        e - jnp.mean(e, axis=1, keepdims=True) - z * jnp.mean(e * z, axis=1, keepdims=True)
    ) * rstd
    grad_ref[...] = grad
    low_ref[...] = grad.astype(BF16)

    @pl.when(pl.program_id(0) == 0)
    def _():
        sum_ref[...] = jnp.zeros_like(sum_ref)

    sum_ref[0:1, :] += jnp.sum(c, axis=0, keepdims=True)
    sum_ref[1:2, :] += jnp.sum(c * z, axis=0, keepdims=True)
    sum_ref[2:3, :] += jnp.sum(grad, axis=0, keepdims=True)


def second_norm(z, feed, c, vectors):
    rows, model = z.shape
    step = rows // 4
    block = pl.BlockSpec((step, model), lambda i: (i, 0))
    return pl.pallas_call(
        second_norm_kernel,
        grid=(4,),
        out_shape=(
            jax.ShapeDtypeStruct((rows, model), BF16),
            jax.ShapeDtypeStruct((rows, model), F32),
            jax.ShapeDtypeStruct((rows, model), BF16),
            jax.ShapeDtypeStruct((8, model), F32),
        ),
        in_specs=[block] * 3 + [VMEM] * 5,
        out_specs=(block, block, block, whole((8, model))),
        compiler_params=params(),
        cost_estimate=COST,
        name="second_norm",
    )(z, feed, c, *vectors)


def first_back_kernel(z_ref, rstd_ref, dn_ref, gain_ref, grad_ref, low_ref, sum_ref):
    z = z_ref[...]
    dn = dn_ref[...]
    f = dn * row(gain_ref)
    grad = (
        f - jnp.mean(f, axis=1, keepdims=True) - z * jnp.mean(f * z, axis=1, keepdims=True)
    ) * rstd_ref[...]
    grad_ref[...] = grad
    low_ref[...] = grad.astype(BF16)

    @pl.when(pl.program_id(0) == 0)
    def _():
        sum_ref[...] = jnp.zeros_like(sum_ref)

    sum_ref[0:1, :] += jnp.sum(dn, axis=0, keepdims=True)
    sum_ref[1:2, :] += jnp.sum(dn * z, axis=0, keepdims=True)
    sum_ref[2:3, :] += jnp.sum(grad, axis=0, keepdims=True)


def first_back(z, rstd, dn, gain):
    rows, model = z.shape
    step = rows // 4
    block = pl.BlockSpec((step, model), lambda i: (i, 0))
    return pl.pallas_call(
        first_back_kernel,
        grid=(4,),
        out_shape=(
            jax.ShapeDtypeStruct((rows, model), F32),
            jax.ShapeDtypeStruct((rows, model), BF16),
            jax.ShapeDtypeStruct((8, model), F32),
        ),
        in_specs=[block, pl.BlockSpec((step, 1), lambda i: (i, 0)), block, VMEM],
        out_specs=(block, block, whole((8, model))),
        compiler_params=params(),
        cost_estimate=COST,
        name="first_back",
    )(z, rstd, dn, gain)


def feed_up_kernel(pieces, count, spot_ref, low_ref, *refs):
    biases, parts, refs = refs[:count], refs[count : count + pieces], refs[count + pieces :]
    if pieces > count:
        win_ref, *refs = refs
        for r in range(4):
            win_ref[quarter(spot_ref, r, parts[r].shape[0]), :] = parts[r][...]
        parts = (win_ref,)
    for n in range(count):
        win_ref, act_ref, slope_ref = parts[n], refs[2 * n], refs[2 * n + 1]
        bias = biases[n][1:2, :].astype(F32)

        @pl.loop(0, low_ref.shape[0] // UP_ROWS)
        def _(i):
            rows = pl.ds(pl.multiple_of(i * UP_ROWS, UP_ROWS), UP_ROWS)
            lifted = dot(low_ref[rows, :], win_ref[...], 1, 0) + bias
            phi_big = 0.5 + 0.5 * lax.erf(lifted * math.sqrt(0.5))
            phi = jnp.exp(-0.5 * lifted * lifted) * (1.0 / math.sqrt(2.0 * math.pi))
            act_ref[rows, :] = (lifted * phi_big).astype(BF16)
            slope_ref[rows, :] = (phi_big + lifted * phi).astype(BF16)


def feed_up(spot, low, parts, biases):
    rows, model = low.shape
    hidden = parts[0].shape[1]
    count = len(biases)
    tall = [jax.ShapeDtypeStruct((model, hidden), BF16)] if len(parts) > count else []
    thin = jax.ShapeDtypeStruct((rows, hidden), BF16)
    return pl.pallas_call(
        functools.partial(feed_up_kernel, len(parts), count),
        out_shape=(*tall, *[thin] * (2 * count)),
        in_specs=[SMEM] + [VMEM] * (1 + count + len(parts)),
        out_specs=(VMEM,) * (2 * count + len(tall)),
        compiler_params=params(),
        cost_estimate=MIDDLE,
        name="feed_up",
    )(spot, low, *biases, *parts)


def feed_down_kernel(pieces, chained, spot_ref, *refs):
    acts, parts, refs = refs[:2], refs[2 : 2 + 2 * pieces], refs[2 + 2 * pieces :]
    if chained:
        acc_ref, *refs = refs
    copies = []
    if pieces > 1:
        *outs, feed_ref, first_ref, second_ref, sems = refs
        wides = (first_ref, second_ref)
        for i in range(2):
            for r, part in enumerate(parts[4 * i : 4 * i + 4]):
                wides[i][quarter(spot_ref, r, part.shape[0]), :] = part[...]
            copies.append(pltpu.make_async_copy(wides[i], outs[i], sems.at[i]))
            copies[-1].start()
    else:
        feed_ref = refs[0]
        wides = parts
    total = dot(acts[0][...], wides[0][...], 1, 0) + dot(acts[1][...], wides[1][...], 1, 0)
    feed_ref[...] = total + acc_ref[...] if chained else total
    for one in copies:
        one.wait()


def feed_down(spot, acts, parts, acc=None):
    rows, hidden = acts[0].shape
    pieces = len(parts[0])
    model = parts[0][0].shape[1]
    more = [] if acc is None else [acc]
    wide = [hbm((hidden, model))] * 2 if pieces > 1 else []
    outs = pl.pallas_call(
        functools.partial(feed_down_kernel, pieces, bool(more)),
        out_shape=(*wide, jax.ShapeDtypeStruct((rows, model), F32)),
        in_specs=[SMEM] + [VMEM] * (2 + 2 * pieces + len(more)),
        out_specs=(HBM,) * len(wide) + (VMEM,),
        scratch_shapes=[pltpu.VMEM(one.shape, one.dtype) for one in wide]
        + ([pltpu.SemaphoreType.DMA((2,))] if wide else []),
        compiler_params=params(),
        cost_estimate=LONG,
        name="feed_down",
    )(spot, *acts, *parts[0], *parts[1], *more)
    return outs if wide else (parts[0][0], parts[1][0], outs[0])


def give_quarters(spot_ref, held_ref, add_ref, first, outs):
    size = held_ref.shape[0] // 4
    for r, (ref, part) in enumerate(outs):
        value = held_ref[quarter(spot_ref, r, size), :]
        if add_ref is not None:
            value = value + add_ref[first + r].astype(F32)
        ref[part] = value.astype(BF16)


TOGETHER = [[(0, r) for r in range(4)], [(0, 4 + r) for r in range(4)]]
DOWN = [[(0, r) for r in range(4)], [(1, r) for r in range(4)]]
INNER = [[(0, 0), (1, 0), (0, 1), (1, 1)], [(2, 0), (2, 1), (3, 0), (3, 1)]]


def grad_shapes(rows, model, plan):
    places = [place for block in plan for place in block]
    return tuple(
        jax.ShapeDtypeStruct((sum(1 for one, _ in places if one == i), rows // 4, model), BF16)
        for i in range(1 + max(one for one, _ in places))
    )


def down_back_kernel(plan, plus, spot_ref, act_a, act_b, low_ref, *refs):
    add_ref, outs, held_ref = (refs[0] if plus else None), refs[plus:-1], refs[-1]
    for n, act_ref in enumerate((act_a, act_b)):
        held_ref[...] = dot(act_ref[...], low_ref[...], 0, 0)
        give_quarters(spot_ref, held_ref, add_ref, 4 * n, [(outs[i], p) for i, p in plan[n]])


def down_back(spot, acts, low, plan, adds=()):
    rows, model = low.shape
    hidden = acts[0].shape[1]
    grads = grad_shapes(hidden, model, plan)
    return pl.pallas_call(
        functools.partial(down_back_kernel, plan, len(adds)),
        out_shape=grads,
        in_specs=[SMEM] + [VMEM] * (3 + len(adds)),
        out_specs=(VMEM,) * len(grads),
        scratch_shapes=[pltpu.VMEM((hidden, model), F32)],
        compiler_params=params(),
        cost_estimate=LONG if adds else COST,
        name="down_back",
    )(spot, *acts, low, *adds)


def feed_back_kernel(plan, plus, spot_ref, low_ref, turned_ref, acc_ref, *refs):
    blocks, add_ref = (refs[:3], refs[3:6]), (refs[6] if plus else None)
    outs, (dn_ref, db_a, db_b, held_ref, dl_ref) = refs[6 + plus : -5], refs[-5:]
    total = acc_ref[...]
    for n, (wd_ref, slope_ref, win_ref) in enumerate(blocks):
        half = win_ref.shape[1] // 2
        for i in range(2):
            part = slice(i * half, (i + 1) * half)
            dl = dot(low_ref[...], wd_ref[part, :], 1, 1) * slope_ref[:, part].astype(F32)
            (db_a, db_b)[n][0:1, part] = jnp.sum(dl, axis=0, keepdims=True)
            dl_ref[:, part] = dl.astype(BF16)
        held_ref[...] = dot(turned_ref[...], dl_ref[...], 1, 0)
        give_quarters(spot_ref, held_ref, add_ref, 4 * n, [(outs[i], p) for i, p in plan[n]])
        total = total + dot(dl_ref[...], win_ref[...], 1, 1)
    dn_ref[...] = total


def feed_back(spot, low, turned, acc, blocks, plan, adds=()):
    rows, model = low.shape
    hidden = blocks[0][2].shape[1]
    grads = grad_shapes(model, hidden, plan)
    flat = [one for block in blocks for one in block]
    return pl.pallas_call(
        functools.partial(feed_back_kernel, plan, len(adds)),
        out_shape=grads
        + (jax.ShapeDtypeStruct((rows, model), F32),)
        + (jax.ShapeDtypeStruct((8, hidden), F32),) * 2,
        in_specs=[SMEM] + [VMEM] * (9 + len(adds)),
        out_specs=(VMEM,) * (3 + len(grads)),
        scratch_shapes=[pltpu.VMEM((model, hidden), F32), pltpu.VMEM((rows, hidden), BF16)],
        compiler_params=params(),
        cost_estimate=COST if adds else LONG,
        name="feed_back",
    )(spot, low, turned, acc, *flat, *adds)


def after(value, *others):
    return lax.optimization_barrier((value, *others))[0]


def swap(value, axis, size, step):
    return lax.ppermute(value, axis, [(i, i ^ step) for i in range(size)])


def add_kernel(plan, *refs):
    outs = refs[len(refs) - len(plan) :]
    for out_ref, terms in zip(outs, plan):
        total = None
        for n, place in terms:
            value = (refs[n][...] if place is None else refs[n][place]).astype(F32)
            total = value if total is None else total + value
        out_ref[...] = total.astype(BF16)


def add(sums, long=False):
    arrays, plan, shapes = [], [], []
    for terms in sums:
        row = []
        for term in terms:
            value, place = term if isinstance(term, tuple) else (term, None)
            known = [n for n, one in enumerate(arrays) if one is value]
            if not known:
                arrays.append(value)
            row.append((known[0] if known else len(arrays) - 1, place))
        value, place = arrays[row[0][0]], row[0][1]
        shape = value.shape
        if isinstance(place, int):
            shape = shape[1:]
        elif place is not None:
            shape = (place.stop - place.start, *shape[1:])
        plan.append(row)
        shapes.append(jax.ShapeDtypeStruct(shape, BF16))
    return pl.pallas_call(
        functools.partial(add_kernel, plan),
        out_shape=tuple(shapes),
        in_specs=[VMEM] * len(arrays),
        out_specs=(VMEM,) * len(shapes),
        compiler_params=params(),
        cost_estimate=LONG if long else COST,
        name="add",
    )(*arrays)


class Line:
    def __init__(self):
        self.last = None

    def __call__(self, value):
        return value if self.last is None else after(value, self.last)

    def done(self, value):
        self.last = value
        return value

    def adds(self, *sums, long=False):
        first = sums[0][0]
        value, place = first if isinstance(first, tuple) else (first, None)
        tied = self(value)
        sums = [
            [
                (tied, term[1]) if isinstance(term, tuple) and term[0] is value
                else tied if term is value
                else term
                for term in terms
            ]
            for terms in sums
        ]
        outs = add(sums, long)
        self.done(outs[0])
        return outs

    def add(self, *terms):
        return self.adds(terms)[0]


class Group:
    def __init__(self, dp, tensor):
        if dp < 8 or dp & (dp - 1):
            raise ValueError("dp size")
        self.dp, self.tensor = dp, tensor
        self.place = lax.axis_index("dp")

    def core(self, value):
        return swap(value, "tensor", self.tensor, 1)

    def across(self, value):
        return swap(value, "tensor", self.tensor, 2)

    def over(self, number, value):
        return swap(value, "dp", self.dp, 2**number)

    def rest(self, value, line):
        number = 3
        while 2**number < self.dp:
            value = line.add(value, self.over(number, value))
            number += 1
        return value


def local(
    inputs,
    lengths,
    weight_query,
    bias_query,
    weight_key,
    weight_value,
    bias_value,
    weight_out,
    bias_out,
    weight_in,
    bias_in,
    weight_down,
    bias_down,
    first_gain,
    first_shift,
    second_gain,
    second_shift,
    cotangent,
):
    group = Group(lax.axis_size("dp"), lax.axis_size("tensor"))
    core, across, over = group.core, group.across, group.over
    width = weight_query.shape[1]
    seq = lax.axis_index("tensor").reshape(1)
    spot = group.place.reshape(1)
    scalars = (lengths, seq, spot)
    line = Line()

    pack, pack_0, pack_3 = prepare_pack(
        spot, weight_query, weight_key, weight_value, weight_out, bias_query, bias_value, bias_in
    )
    line.done(pack_0)
    far_0 = across(pack_0)
    pack_twin = core(pack)
    win_0, win_3, wd_0, wd_3 = prepare_feed(line(spot), weight_in, weight_down)
    line.done(win_0)
    kept = [None] * 4
    kept[0] = attend_forward(scalars, line(inputs), [pack])
    line.done(kept[0][4])
    far_3 = across(line(pack_3))
    kept[1] = attend_forward(scalars, line(inputs), [pack_twin])
    line.done(kept[1][4])
    far_0 = line.done(line(far_0))
    far_1, far_2 = over(1, far_0), over(0, far_0)
    win_0 = across(after(win_0, far_0))
    far_3 = line.done(line(far_3))
    far_parts = [far_0, far_1, far_2, far_3]
    pack_twin = [core(one) for one in far_parts]
    kept[2] = attend_forward(scalars, line(inputs), far_parts)
    line.done(kept[2][4])
    wd_0 = across(after(wd_0, kept[2][4]))
    win_0 = line.done(line(win_0))
    win_1, win_2 = over(1, win_0), over(0, win_0)
    win_3 = across(after(win_3, win_0))
    kept[3] = attend_forward(scalars, line(inputs), pack_twin)
    line.done(kept[3][4])
    win_twin = core(after(weight_in, kept[2][4]))
    z, low, turned, rstd = first_norm(
        line(inputs),
        (bias_out, first_gain, first_shift),
        [one[4] for one in kept],
        [one[0] for one in kept],
    )
    line.done(low)
    acts, slopes = [None] * 4, [None] * 4
    acts[0], slopes[0], acts[1], slopes[1] = feed_up(
        spot, line(low), [weight_in, win_twin], [kept[0][5], kept[1][5]]
    )
    line.done(acts[0])
    wd_0 = line.done(line(wd_0))
    wd_1, wd_2 = over(1, wd_0), over(0, wd_0)
    wd_3 = across(after(wd_3, wd_0))
    wd_twin = core(after(weight_down, kept[3][4]))
    win_far, acts[2], slopes[2] = feed_up(
        spot, line(low), [win_0, win_1, win_2, win_3], [kept[2][5]]
    )
    line.done(acts[2])
    wins = [weight_in, win_twin, win_far, core(win_far)]
    wd_parts = [wd_0, wd_1, wd_2, wd_3]
    *near, feed = feed_down(spot, [line(acts[0]), acts[1]], [[weight_down], [wd_twin]])
    line.done(feed)
    wd_twin = [core(one) for one in wd_parts]
    acts[3], slopes[3] = feed_up(spot, line(low), [wins[3]], [kept[3][5]])
    line.done(acts[3])
    *far, feed = feed_down(spot, [line(acts[2]), acts[3]], [wd_parts, wd_twin], feed)
    wds = near + far
    results, grad_second, second_low, second_sums = second_norm(
        z, feed, cotangent, (first_gain, first_shift, bias_down, second_gain, second_shift)
    )
    line.done(second_low)

    def down(pair, plan, adds=()):
        grads = down_back(spot, [acts[r] for r in pair], line(second_low), plan, adds)
        line.done(grads[0])
        return grads

    db = [None] * 4

    def back(pair, acc, plan, adds=()):
        blocks = [(wds[r], slopes[r], wins[r]) for r in pair]
        *grads, acc, db[pair[0]], db[pair[1]] = feed_back(
            spot, line(second_low), turned, acc, blocks, plan, adds
        )
        line.done(acc)
        return grads, acc

    (down_twin,) = down((3, 1), TOGETHER)
    down_twin = core(down_twin)
    (win_twin,), dn = back((3, 1), grad_second, TOGETHER)
    win_twin = core(win_twin)
    down_far, down_near = down((2, 0), DOWN, [down_twin])
    down_far = across(down_far)
    (far_keep, far_send, near_keep, near_send), dn = back((2, 0), dn, INNER, [win_twin])
    far_moved, near_moved = over(1, far_send), over(0, near_send)
    grad_first, first_low, first_sums = first_back(line(z), rstd, dn, first_gain)
    line.done(first_low)
    gs = [None] * 4

    def attention_back(blocks, split=False, adds=()):
        outs = attend_backward(
            spot,
            inputs,
            line(first_low),
            [db[r] for r in blocks],
            first_sums,
            second_sums,
            [kept[r][:5] for r in blocks],
            split,
            adds,
        )
        for r, one in zip(blocks, outs[-len(blocks) :]):
            gs[r] = one
        line.done(gs[blocks[-1]])
        return outs[: -len(blocks)]

    (pack_twin,) = attention_back((3, 1))
    pack_twin = core(pack_twin)

    def input_part(acc, pair):
        part = input_grad(line(acc), [gs[r] for r in pair], [kept[r][0] for r in pair])
        return line.done(part)

    dx = input_part(grad_first, (3, 1))
    down_s, down_1, down_0, win_f2, win_n1 = line.adds(
        [(down_near, slice(2, 4)), (down_far, slice(2, 4))],
        [(down_near, 1), (down_far, 1)],
        [(down_near, 0), (down_far, 0)],
        [(far_keep, 1), (far_moved, 1)],
        [(near_keep, 1), (near_moved, 1)],
        long=True,
    )
    win_fx, win_nz, down_x = over(0, win_f2), over(1, win_n1), over(0, down_s)
    pack_0, pack_321 = attention_back((2,), True, [pack_twin])
    pack_321 = across(pack_321)
    (pack_near,) = attention_back((0,), False, [pack_twin])
    dx = input_part(dx, (2, 0))
    win_f0, win_0, down_1, down_0 = line.adds(
        [(far_keep, 0), (far_moved, 0), win_fx],
        [(near_keep, 0), (near_moved, 0), win_nz],
        [down_1, (down_x, 1)],
        [down_0, (down_x, 0)],
    )
    down_z, win_y = over(1, down_1), across(win_f0)
    pack_0 = across(after(pack_0, win_f0))
    down_0 = line.add(down_0, down_z)
    down_far = over(2, down_0)
    pack_x = [
        over(0, one)
        for one in line.adds(
            [(pack_near, 3), (pack_321, 1)], [(pack_near, 2), (pack_321, 0)]
        )
    ]
    win_0 = line.add(win_0, win_y)
    win_far = over(2, win_0)
    down_0 = group.rest(line.add(down_0, down_far), line)
    down_1, down_2 = over(1, down_0), over(0, down_0)
    pack_1, pack_0 = line.adds(
        [(pack_near, 1), (pack_321, 2), pack_x[0]], [(pack_near, 0), pack_0, pack_x[1]]
    )
    pack_z = over(1, pack_1)
    down_1 = line.done(line(down_1))
    down_3 = over(0, down_1)
    win_0 = group.rest(line.add(win_0, win_far), line)
    win_1, win_2 = over(1, win_0), over(0, win_0)
    pack_0 = line.add(pack_0, pack_z)
    pack_far = over(2, pack_0)
    grad_weight_down = finish_block(line(spot), [down_0, down_1, down_2, down_3])
    line.done(grad_weight_down)
    win_1 = line.done(line(win_1))
    win_3 = over(0, win_1)
    win_2 = line.done(line(win_2))
    pack_0 = group.rest(line.add(pack_0, pack_far), line)
    pack_1, pack_2 = over(1, pack_0), over(0, pack_0)
    grad_weight_in = finish_block(line(spot), [win_0, win_1, win_2, win_3])
    line.done(grad_weight_in)
    parts = [pack_0, pack_1, pack_2, over(0, pack_1)]
    grad_q, grad_k, grad_v, grad_o, extra = finish_pack(line(spot), parts, width)
    return (
        results,
        dx,
        grad_q.T,
        extra[0, :width],
        grad_k.T,
        grad_v.T,
        extra[0, 2 * width : 3 * width],
        grad_o,
        extra[4],
        grad_weight_in,
        extra[1],
        grad_weight_down,
        extra[7],
        extra[3],
        extra[2],
        extra[6],
        extra[5],
    )


def solution(mesh):
    in_specs = (
        P(("dp", "tensor"), None),
        P("dp"),
        P(None, "tensor"),
        P("tensor"),
        P(None, "tensor"),
        P(None, "tensor"),
        P("tensor"),
        P("tensor", None),
        P(),
        P(None, "tensor"),
        P("tensor"),
        P("tensor", None),
        P(),
        P(),
        P(),
        P(),
        P(),
        P(("dp", "tensor"), None),
    )
    out_specs = (
        P(("dp", "tensor"), None),
        P(("dp", "tensor"), None),
        P(None, "tensor"),
        P("tensor"),
        P(None, "tensor"),
        P(None, "tensor"),
        P("tensor"),
        P("tensor", None),
        P(),
        P(None, "tensor"),
        P("tensor"),
        P("tensor", None),
        P(),
        P(),
        P(),
        P(),
        P(),
    )
    return jax.shard_map(local, mesh=mesh, in_specs=in_specs, out_specs=out_specs, check_vma=False)
```

time: 740 us -> 226 us (0.31)
  waiting for transfers between devices: 462 us -> 72.7 us
  matrix products: 100 us -> 0 us
  Pallas kernels: 0 us -> 95.8 us
  blocking collectives: 64.1 us -> 0 us
  starting transfers between devices: 1.53 us -> 51.6 us
  local copies, waits for them, and re-layouts: 45.9 us -> 1.4 us
  other arithmetic: 42.3 us -> 0 us
  between operations: 14.6 us -> 1.66 us
    psum x1 -> x0, waiting for transfers between devices: 199 us -> none  [local(): lax.psum((grad_weight_query, grad_bias_query, grad_weight_key, grad_weigh...]
    reduce_scatter x4 -> x0, waiting for transfers between devices: 151 us -> none  [the longest x1 58.5 us: local(): lax.psum_scatter(contract_cols(lifted_low, weight_in), 'tensor', scatter_...]
    all_gather x4 -> x0, waiting for transfers between devices: 112 us -> none  [the longest x1 28.6 us: local(): gathered = lax.all_gather(inputs, 'tensor', axis=0, tiled=True)]
    dot_general x40 -> x0, matrix products: 100 us -> none  [the longest x4 22.6 us: contract_cols(): lax.dot_general(left, right, (((1,), (1,)), ((), ())), preferred_element_...]
    pallas_call x0 -> x36, Pallas kernels: none -> 95.8 us  [the longest x3 21.3 us: attend_backward(): pl.pallas_call(functools.partial(attend_backward_kernel, count, len(more)...]
    ppermute x0 -> x52, waiting for transfers between devices: none -> 72.7 us  [swap(): return lax.ppermute(value, axis, [(i, i ^ step) for i in range(size)])]
    psum x2 -> x0, blocking collectives: 64.1 us -> none  [the longest x1 40.4 us: local(): lax.psum((grad_bias_out, grad_bias_down, grad_first_gain, grad_first_shif...]
    ppermute x0 -> x52, starting transfers between devices: none -> 51.6 us  [swap(): return lax.ppermute(value, axis, [(i, i ^ step) for i in range(size)])]
  transfers between devices with their start and end apart: 9 -> 52, of which waited for: 8 -> 21; matrix products, arithmetic and copies ran while one was open for 4% -> 0% of each run, Pallas kernels for 0% -> 38%
where the time goes in v1:
time: 226 us; the launch traced here: 223 us
  Pallas kernels  95.8 us (42%)
  waiting for transfers between devices  72.7 us (32%)
  starting transfers between devices  51.6 us (23%)
    ppermute x52, waiting for transfers between devices, swap(): return lax.ppermute(value, axis, [(i, i ^ step) for i in range(size)])  72.7 us
    ppermute x52, starting transfers between devices, swap(): return lax.ppermute(value, axis, [(i, i ^ step) for i in range(size)])  51.6 us
    pallas_call x3, Pallas kernels, attend_backward(): pl.pallas_call(functools.partial(attend_backward_kernel, count, len(more)...  21.3 us
    pallas_call x4, Pallas kernels, attend_forward(): pl.pallas_call(functools.partial(attend_forward_kernel, pieces), out_shap...  14.8 us
    pallas_call x2, Pallas kernels, feed_back(): pl.pallas_call(functools.partial(feed_back_kernel, plan, len(adds)), out_...  10.4 us
    pallas_call x1, Pallas kernels, first_back(): pl.pallas_call(first_back_kernel, grid=(4,), out_shape=(jax.ShapeDtypeStr...  10.1 us
    pallas_call x2, Pallas kernels, input_grad(): pl.pallas_call(functools.partial(input_grad_kernel, count), out_shape=jax...  8.24 us
    pallas_call x3, Pallas kernels, feed_up(): pl.pallas_call(functools.partial(feed_up_kernel, len(parts), count), out_...  6.83 us
  transfers between devices with their start and end apart: 52, of which 21 were waited for; matrix products, arithmetic and copies ran while one was open for 0% of the time, Pallas kernels for 38%

profile of v1, /device:TPU:0, one launch (start us, length us, event | category | flops | bytes accessed | tf_op | source)
XLA Modules:
  0.0 223.3 jit_solution(10358700097697116461)
XLA Ops:
  0.7 2.7 %prepare_pack.1 = (bf16[832,768]{1,0:T(8,128)(2,1)}, bf16[208,768]{1,0:T(8,128)(2,1)}, bf16[208,768]{1,0:T(8,128)(2,1)}) custom-call(s32[1]{0:T(128)} %bitcast.1.spot_ref, bf16[192,768]{1,0:T(8,128)(2,1)} %bitcast.10, bf16[192,768]{1,0:T(8,128)(2,1)} %bitcast.11, bf16[192,768]{1,0:T(8,128)(2,1)} %bitcast.12, bf16[192,768]{1,0:T(8,128)(2,1)} %out_ref.1, ...), custom_call_target="tpu_custom_call" | custom-call | tf_op jit(solution)/shard_map/prepare_pack/pallas_call | solution.py:112
  3.9 2.6 %collective-permute-start = (bf16[208,768]{1,0:T(8,128)(2,1)}, bf16[208,768]{1,0:T(8,128)(2,1)}, u32[]{:S(2)}, u32[]{:S(2)}) collective-permute-start(bf16[208,768]{1,0:T(8,128)(2,1)} %get-tuple-element.157), channel_id=1, source_target_pairs={{0,2},{1,3},{2,0},{3,1},{4,6},{5,7},{6,4},{7,5},{8,10},{9,11},{10,... | collective-permute-start | bytes 958472 | tf_op jit(solution)/shard_map/ppermute | solution.py:730
  6.5 2.0 prepare_feed.1
  8.6 3.6 %attend_forward.4 = (bf16[576,512]{1,0:T(8,128)(2,1)}, bf16[3,512,512]{2,1,0:T(8,128)(2,1)}, f32[8,512]{1,0:T(8,128)}, bf16[192,512]{1,0:T(8,128)(2,1)}, bf16[16,768]{1,0:T(8,128)(2,1)S(1)}) custom-call(s32[4]{0:T(128)S(1)} %copy-done.24, s32[1]{0:T(128)} %bitcast.seq_ref, s32[1]{0:T(128)} %bitcast.1.spot_ref, bf16[512,768]{1,0:T(8,128)(2,1)S(1)} %copy-done.22, ...), custom_call_target="tpu_custom_call" | custom-call | flops 10000000000 | bytes 1000000000 | tf_op jit(solution)/shard_map/attend_forward/pallas_call | solution.py:261
  12.4 3.6 %attend_forward.5 = (bf16[576,512]{1,0:T(8,128)(2,1)}, bf16[3,512,512]{2,1,0:T(8,128)(2,1)}, f32[8,512]{1,0:T(8,128)}, bf16[192,512]{1,0:T(8,128)(2,1)}, bf16[16,768]{1,0:T(8,128)(2,1)S(1)}) custom-call(s32[4]{0:T(128)S(1)} %copy-done.24, s32[1]{0:T(128)} %bitcast.seq_ref, s32[1]{0:T(128)} %bitcast.1.spot_ref, bf16[512,768]{1,0:T(8,128)(2,1)S(1)} %copy-done.22, ...), custom_call_target="tpu_custom_call" | custom-call | flops 10000000000 | bytes 1000000000 | tf_op jit(solution)/shard_map/attend_forward/pallas_call | solution.py:261
  16.0 1.9 collective-permute-start.5
  18.0 1.6 collective-permute-start.4
  19.5 2.3 %collective-permute-done.3.refs_3_ = bf16[208,768]{1,0:T(8,128)(2,1)S(1)} collective-permute-done((bf16[208,768]{1,0:T(8,128)(2,1)S(1)}, bf16[208,768]{1,0:T(8,128)(2,1)S(1)}, u32[]{:S(2)}, u32[]{:S(2)}) %collective-permute-start.3) | collective-permute-done | bytes 319520 | tf_op jit(solution)/shard_map/ppermute | solution.py:730
  22.4 1.6 collective-permute-start.2
  24.0 1.8 collective-permute-done.5.refs_2_
  25.8 1.4 collective-permute-done.4.refs_1_
  27.2 4.0 %attend_forward.6 = (bf16[832,768]{1,0:T(8,128)(2,1)}, bf16[576,512]{1,0:T(8,128)(2,1)}, bf16[3,512,512]{2,1,0:T(8,128)(2,1)}, f32[8,512]{1,0:T(8,128)}, bf16[19...) custom-call(s32[4]{0:T(128)S(1)} %copy-done.24, s32[1]{0:T(128)} %bitcast.seq_ref, s32[1]{0:T(128)} %bitcast.1.spot_ref, ...), custom_call_target="tpu_custom_call" | custom-call | flops 10000000000 | bytes 1000000000 | tf_op jit(solution)/shard_map/attend_forward/pallas_call | solution.py:261
  31.3 1.6 collective-permute-start.13
  32.9 1.6 collective-permute-start.12
  34.5 1.5 collective-permute-start.14
  36.6 3.6 %attend_forward.7 = (bf16[832,768]{1,0:T(8,128)(2,1)}, bf16[576,512]{1,0:T(8,128)(2,1)}, bf16[3,512,512]{2,1,0:T(8,128)(2,1)}, f32[8,512]{1,0:T(8,128)}, bf16[19...) custom-call(s32[4]{0:T(128)S(1)} %copy-done.24, s32[1]{0:T(128)} %bitcast.seq_ref, s32[1]{0:T(128)} %bitcast.1.spot_ref, ...), custom_call_target="tpu_custom_call" | custom-call | flops 10000000000 | bytes 1000000000 | tf_op jit(solution)/shard_map/attend_forward/pallas_call | solution.py:261
  40.2 3.1 %first_norm.1 = (f32[512,768]{1,0:T(8,128)S(1)}, bf16[512,768]{1,0:T(8,128)(2,1)S(1)}, bf16[768,512]{1,0:T(8,128)(2,1)S(1)}, f32[512,1]{1,0:T(8,128)S(1)}) custom-call(bf16[512,768]{1,0:T(8,128)(2,1)S(1)} %copy-done.22, bf16[768]{0:T(1024)(128)(2,1)S(1)} %copy-done.23, bf16[768]{0:T(1024)(128)(2,1)S(1)} %copy-done.17, bf16[768]{0:T(1024)(128)(2,1)S(1)} %copy-done.12, ...), custom_call_target="tpu_custom_call" | custom-call | flops 10000000000 | bytes 1000000000 | tf_op jit(solution)/shard_map/first_norm/pallas_call | solution.py:458
  43.9 3.5 %feed_up.3 = (bf16[512,768]{1,0:T(8,128)(2,1)S(1)}, bf16[512,768]{1,0:T(8,128)(2,1)S(1)}, bf16[512,768]{1,0:T(8,128)(2,1)S(1)}, bf16[512,768]{1,0:T(8,128)(2,1)S(1)}) custom-call(s32[1]{0:T(128)} %bitcast.1.spot_ref, bf16[512,768]{1,0:T(8,128)(2,1)S(1)} %get-tuple-element.196.low_ref, bf16[16,768]{1,0:T(8,128)(2,1)S(1)} %get-tuple-element.183.refs_0_, ...), custom_call_target="tpu_custom_call" | custom-call | flops 10000000000 | bytes 1000000000 | tf_op jit(solution)/shard_map/feed_up/pallas_call | solution.py:591
  48.7 1.5 collective-permute-start.18
  50.7 1.5 collective-permute-start.19
  52.2 1.7 feed_up.4
  53.9 5.6 %collective-permute-done.19.refs_5_ = bf16[192,768]{1,0:T(8,128)(2,1)S(1)} collective-permute-done((bf16[192,768]{1,0:T(8,128)(2,1)S(1)}, bf16[192,768]{1,0:T(8,128)(2,1)S(1)}, u32[]{:S(2)}, u32[]{:S(2)}) %collective-permute-start.19) | collective-permute-done | bytes 294944 | tf_op jit(solution)/shard_map/ppermute | solution.py:730
  60.6 1.4 feed_down.2.refs_10_
  62.4 1.6 feed_up.5
  64.1 2.3 %feed_down.3 = (bf16[768,768]{1,0:T(8,128)(2,1)}, bf16[768,768]{1,0:T(8,128)(2,1)}, f32[512,768]{1,0:T(8,128)S(1)}) custom-call(s32[1]{0:T(128)} %bitcast.1.spot_ref, bf16[512,768]{1,0:T(8,128)(2,1)S(1)} %get-tuple-element.200.refs_0_.act_a, bf16[512,768]{1,0:T(8,128)(2,1)S(1)} %get-tuple-element.199.refs_1_.act_a, ...), custom_call_target="tpu_custom_call" | custom-call | flops 99999997952 | bytes 1000000000 | tf_op jit(solution)/shard_map/feed_down/pallas_call | solution.py:630
  66.5 2.6 %second_norm.1 = (bf16[512,768]{1,0:T(8,128)(2,1)}, f32[512,768]{1,0:T(8,128)S(1)}, bf16[512,768]{1,0:T(8,128)(2,1)S(1)}, f32[8,768]{1,0:T(8,128)S(1)}) custom-call(f32[512,768]{1,0:T(8,128)S(1)} %get-tuple-element.222.z_ref, f32[512,768]{1,0:T(8,128)S(1)} %get-tuple-element.203.feed_ref, bf16[512,768]{1,0:T(8,128)(2,1)S(1)} %copy-done.11, ...), custom_call_target="tpu_custom_call" | custom-call | flops 1000000000 | bytes 1000000000 | tf_op jit(solution)/shard_map/second_norm/pallas_call | solution.py:508
  69.1 1.8 down_back.2
  71.2 5.1 %feed_back.2 = (bf16[8,192,768]{2,1,0:T(8,128)(2,1)S(1)}, f32[512,768]{1,0:T(8,128)S(1)}, f32[8,768]{1,0:T(8,128)S(1)}, f32[8,768]{1,0:T(8,128)S(1)}) custom-call(s32[1]{0:T(128)} %bitcast.1.spot_ref, bf16[512,768]{1,0:T(8,128)(2,1)S(1)} %get-tuple-element.216.low_ref, bf16[768,512]{1,0:T(8,128)(2,1)S(1)} %get-tuple-element.208.turned_ref, ...), custom_call_target="tpu_custom_call" | custom-call | flops 99999997952 | bytes 1000000000 | tf_op jit(solution)/shard_map/feed_back/pallas_call | solution.py:711
  76.7 2.0 down_back.3
  78.7 1.6 collective-permute-start.26
  80.9 5.3 %feed_back.3 = (bf16[2,192,768]{2,1,0:T(8,128)(2,1)S(1)}, bf16[2,192,768]{2,1,0:T(8,128)(2,1)S(1)}, bf16[2,192,768]{2,1,0:T(8,128)(2,1)S(1)}, bf16[2,192,768]{2,...) custom-call(s32[1]{0:T(128)} %bitcast.1.spot_ref, ...), custom_call_target="tpu_custom_call" | custom-call | flops 1000000000 | bytes 1000000000 | tf_op jit(solution)/shard_map/feed_back/pallas_call | solution.py:711
  86.3 10.1 %first_back.1 = (f32[512,768]{1,0:T(8,128)S(1)}, bf16[512,768]{1,0:T(8,128)(2,1)S(1)}, f32[8,768]{1,0:T(8,128)S(1)}) custom-call(f32[512,768]{1,0:T(8,128)S(1)} %copy-done.5, f32[512,1]{1,0:T(8,128)S(1)} %get-tuple-element.223.rstd_ref, f32[512,768]{1,0:T(8,128)S(1)} %get-tuple-element.221.dn_ref, bf16[768]{0:T(1024)(128)(2,1)S(1)} %copy-done.19), custom_call_target="tpu_custom_call" | custom-call | flops 1000000000 | bytes 1000000000 | tf_op jit(solution)/shard_map/first_back/pallas_call | solution.py:548
  96.4 1.7 collective-permute-start.27
  98.6 9.5 %attend_backward.3 = (bf16[8,208,768]{2,1,0:T(8,128)(2,1)}, bf16[576,512]{1,0:T(8,128)(2,1)}, bf16[576,512]{1,0:T(8,128)(2,1)}) custom-call(s32[1]{0:T(128)} %bitcast.1.spot_ref, bf16[512,768]{1,0:T(8,128)(2,1)S(1)} %copy-done.22, bf16[512,768]{1,0:T(8,128)(2,1)S(1)} %get-tuple-element.254.bg_ref, f32[8,768]{1,0:T(8,128)S(1)} %get-tuple-element.227.refs_0_, ...), custom_call_target="tpu_custom_call" | custom-call | flops 10000000000 | bytes 1000000000 | tf_op jit(solution)/shard_map/attend_backward/pallas_call | solution.py:367
  108.1 3.5 %input_grad.2.acc_ref = f32[512,768]{1,0:T(8,128)S(1)} custom-call(f32[512,768]{1,0:T(8,128)S(1)} %get-tuple-element.238.acc_ref, bf16[576,512]{1,0:T(8,128)(2,1)} %get-tuple-element.239.refs_0_, bf16[576,512]{1,0:T(8,128)(2,1)} %get-tuple-element.237.refs_1_, bf16[832,768]{1,0:T(8,128)(2,1)} %get-tuple-element.177.refs_7_.refs_4_.refs_2_, ...), custom_call_target="tpu_custom_call" | custom-call | flops 1000000000 | bytes 1000000000 | tf_op jit(solution)/shard_map/input_grad/pallas_call | solution.py:415
  112.1 1.3 collective-permute-done.28.refs_5_.refs_4_
  114.4 1.5 collective-permute-start.30
  116.5 5.9 %attend_backward.4 = (bf16[208,768]{1,0:T(8,128)(2,1)}, bf16[3,208,768]{2,1,0:T(8,128)(2,1)}, bf16[576,512]{1,0:T(8,128)(2,1)}) custom-call(s32[1]{0:T(128)} %bitcast.1.spot_ref, bf16[512,768]{1,0:T(8,128)(2,1)S(1)} %copy-done.22, bf16[512,768]{1,0:T(8,128)(2,1)S(1)} %get-tuple-element.254.bg_ref, f32[8,768]{1,0:T(8,128)S(1)} %get-tuple-element.248.refs_0_, ...), custom_call_target="tpu_custom_call" | custom-call | flops 10000000000 | bytes 1000000000 | tf_op jit(solution)/shard_map/attend_backward/pallas_call | solution.py:367
  122.4 1.6 collective-permute-start.34
  124.0 5.9 %attend_backward.5 = (bf16[4,208,768]{2,1,0:T(8,128)(2,1)}, bf16[576,512]{1,0:T(8,128)(2,1)}) custom-call(s32[1]{0:T(128)} %bitcast.1.spot_ref, bf16[512,768]{1,0:T(8,128)(2,1)S(1)} %copy-done.22, bf16[512,768]{1,0:T(8,128)(2,1)S(1)} %get-tuple-element.254.bg_ref, f32[8,768]{1,0:T(8,128)S(1)} %get-tuple-element.255.refs_0_, ...), custom_call_target="tpu_custom_call" | custom-call | flops 10000000000 | bytes 1000000000 | tf_op jit(solution)/shard_map/attend_backward/pallas_call | solution.py:367
  129.9 4.7 %input_grad.3 = f32[512,768]{1,0:T(8,128)} custom-call(f32[512,768]{1,0:T(8,128)S(1)} %input_grad.2.acc_ref, bf16[576,512]{1,0:T(8,128)(2,1)} %get-tuple-element.253.refs_0_, bf16[576,512]{1,0:T(8,128)(2,1)} %get-tuple-element.259.refs_1_, bf16[832,768]{1,0:T(8,128)(2,1)} %get-tuple-element.176.refs_6_.refs_3_.refs_2_, ...), custom_call_target="tpu_custom_call" | custom-call | flops 1000000000 | bytes 1000000000 | tf_op jit(solution)/shard_map/input_grad/pallas_call | solution.py:415
  135.0 1.5 collective-permute-start.33
  137.2 1.4 collective-permute-start.38
  138.5 5.3 %collective-permute-done.33.refs_1_ = bf16[192,768]{1,0:T(8,128)(2,1)S(1)} collective-permute-done((bf16[192,768]{1,0:T(8,128)(2,1)S(1)}, bf16[192,768]{1,0:T(8,128)(2,1)S(1)}, u32[]{:S(2)}, u32[]{:S(2)}) %collective-permute-start.33) | collective-permute-done | bytes 294944 | tf_op jit(solution)/shard_map/ppermute | solution.py:730
  143.9 3.0 %collective-permute-start.36 = (bf16[192,768]{1,0:T(8,128)(2,1)S(1)}, bf16[192,768]{1,0:T(8,128)(2,1)S(1)}, u32[]{:S(2)}, u32[]{:S(2)}) collective-permute-start(bf16[192,768]{1,0:T(8,128)(2,1)S(1)} %add.19.refs_0_), channel_id=1, source_target_pairs={{0,16},{4,20},{8,24},{12,28},{16,0},{20,4},{24,8},{28,12},{1,17},{... | collective-permute-start | bytes 884744 | tf_op jit(solution)/shard_map/ppermute | solution.py:730
  147.1 1.4 collective-permute-start.39
  149.2 3.9 %collective-permute-done.35.refs_1_ = bf16[192,768]{1,0:T(8,128)(2,1)S(1)} collective-permute-done((bf16[192,768]{1,0:T(8,128)(2,1)S(1)}, bf16[192,768]{1,0:T(8,128)(2,1)S(1)}, u32[]{:S(2)}, u32[]{:S(2)}) %collective-permute-start.35) | collective-permute-done | bytes 294944 | tf_op jit(solution)/shard_map/ppermute | solution.py:730
  153.2 5.4 %collective-permute-done.36.refs_1_ = bf16[192,768]{1,0:T(8,128)(2,1)S(1)} collective-permute-done((bf16[192,768]{1,0:T(8,128)(2,1)S(1)}, bf16[192,768]{1,0:T(8,128)(2,1)S(1)}, u32[]{:S(2)}, u32[]{:S(2)}) %collective-permute-start.36) | collective-permute-done | bytes 294944 | tf_op jit(solution)/shard_map/ppermute | solution.py:730
  158.7 2.7 %collective-permute-start.41 = (bf16[192,768]{1,0:T(8,128)(2,1)S(1)}, bf16[192,768]{1,0:T(8,128)(2,1)S(1)}, u32[]{:S(2)}, u32[]{:S(2)}) collective-permute-start(bf16[192,768]{1,0:T(8,128)(2,1)S(1)} %add.21.refs_0_), channel_id=1, source_target_pairs={{0,16},{4,20},{8,24},{12,28},{16,0},{20,4},{24,8},{28,12},{1,17},{... | collective-permute-start | bytes 884744 | tf_op jit(solution)/shard_map/ppermute | solution.py:730
  162.3 1.9 collective-permute-start.45
  164.2 10.6 %collective-permute-done.40.refs_1_ = bf16[192,768]{1,0:T(8,128)(2,1)S(1)} collective-permute-done((bf16[192,768]{1,0:T(8,128)(2,1)S(1)}, bf16[192,768]{1,0:T(8,128)(2,1)S(1)}, u32[]{:S(2)}, u32[]{:S(2)}) %collective-permute-start.40) | collective-permute-done | bytes 294944 | tf_op jit(solution)/shard_map/ppermute | solution.py:730
  174.9 2.0 collective-permute-start.46
  176.9 3.9 %collective-permute-done.42.refs_1_ = bf16[208,768]{1,0:T(8,128)(2,1)S(1)} collective-permute-done((bf16[208,768]{1,0:T(8,128)(2,1)S(1)}, bf16[208,768]{1,0:T(8,128)(2,1)S(1)}, u32[]{:S(2)}, u32[]{:S(2)}) %collective-permute-start.42) | collective-permute-done | bytes 319520 | tf_op jit(solution)/shard_map/ppermute | solution.py:730
  181.6 3.4 %collective-permute-start.43 = (bf16[192,768]{1,0:T(8,128)(2,1)S(1)}, bf16[192,768]{1,0:T(8,128)(2,1)S(1)}, u32[]{:S(2)}, u32[]{:S(2)}) collective-permute-start(bf16[192,768]{1,0:T(8,128)(2,1)S(1)} %add.24.refs_0_), channel_id=1, source_target_pairs={{0,4},{4,0},{8,12},{12,8},{16,20},{20,16},{24,28},{28,24},{1,5},{5... | collective-permute-start | bytes 884744 | tf_op jit(solution)/shard_map/ppermute | solution.py:730
  185.0 1.6 finish_block.2
  186.6 7.1 %collective-permute-done.44.refs_1_ = bf16[192,768]{1,0:T(8,128)(2,1)S(1)} collective-permute-done((bf16[192,768]{1,0:T(8,128)(2,1)S(1)}, bf16[192,768]{1,0:T(8,128)(2,1)S(1)}, u32[]{:S(2)}, u32[]{:S(2)}) %collective-permute-start.44) | collective-permute-done | bytes 294944 | tf_op jit(solution)/shard_map/ppermute | solution.py:730
  193.7 3.6 %collective-permute-done.47.refs_1_ = bf16[208,768]{1,0:T(8,128)(2,1)S(1)} collective-permute-done((bf16[208,768]{1,0:T(8,128)(2,1)S(1)}, bf16[208,768]{1,0:T(8,128)(2,1)S(1)}, u32[]{:S(2)}, u32[]{:S(2)}) %collective-permute-start.47) | collective-permute-done | bytes 319520 | tf_op jit(solution)/shard_map/ppermute | solution.py:730
  197.4 2.0 collective-permute-start.48
  199.5 7.2 %collective-permute-done.49.refs_1_ = bf16[208,768]{1,0:T(8,128)(2,1)S(1)} collective-permute-done((bf16[208,768]{1,0:T(8,128)(2,1)S(1)}, bf16[208,768]{1,0:T(8,128)(2,1)S(1)}, u32[]{:S(2)}, u32[]{:S(2)}) %collective-permute-start.49) | collective-permute-done | bytes 319520 | tf_op jit(solution)/shard_map/ppermute | solution.py:730
  206.8 2.0 collective-permute-start.51
  208.8 1.6 finish_block.3
  210.3 3.9 %collective-permute-done.50.refs_2_ = bf16[208,768]{1,0:T(8,128)(2,1)S(1)} collective-permute-done((bf16[208,768]{1,0:T(8,128)(2,1)S(1)}, bf16[208,768]{1,0:T(8,128)(2,1)S(1)}, u32[]{:S(2)}, u32[]{:S(2)}) %collective-permute-start.50) | collective-permute-done | bytes 319520 | tf_op jit(solution)/shard_map/ppermute | solution.py:730
  214.2 6.1 %collective-permute-done.51.refs_3_ = bf16[208,768]{1,0:T(8,128)(2,1)S(1)} collective-permute-done((bf16[208,768]{1,0:T(8,128)(2,1)S(1)}, bf16[208,768]{1,0:T(8,128)(2,1)S(1)}, u32[]{:S(2)}, u32[]{:S(2)}) %collective-permute-start.51) | collective-permute-done | bytes 319520 | tf_op jit(solution)/shard_map/ppermute | solution.py:730
  220.3 1.5 finish_pack.1
  (150 shorter events, 15.1 us)
Async XLA Ops:
  0.7 7.9 %copy-start.22 = (bf16[512,768]{1,0:T(8,128)(2,1)S(1)}, bf16[512,768]{1,0:T(8,128)(2,1)}, u32[]{:S(2)}) copy-start(bf16[512,768]{1,0:T(8,128)(2,1)} %x_ref.10) | copy-start | bytes 2359300
  0.7 7.9 %copy-start.24 = (s32[4]{0:T(128)S(1)}, s32[4]{0:T(128)}, u32[]{:S(2)}) copy-start(s32[4]{0:T(128)} %length_ref.7) | copy-start | bytes 52
  3.4 9.0 %collective-permute-start.1 = (bf16[832,768]{1,0:T(8,128)(2,1)}, bf16[832,768]{1,0:T(8,128)(2,1)S(1)}, u32[]{:S(2)}, u32[]{:S(2)}) collective-permute-start(bf16[832,768]{1,0:T(8,128)(2,1)} %get-tuple-element.161.refs_0_.refs_4_.refs_3_), channel_id=1, source_target_pairs={{0,1},{1,0},{2,3},{3,2},{4,5},{5,4},{6,7},{7,6},{8,9},{9,8},{10,11... | collective-permute-start | bytes 3833864 | tf_op jit(solution)/shard_map/ppermute | solution.py:730
  3.9 12.1 %collective-permute-start = (bf16[208,768]{1,0:T(8,128)(2,1)}, bf16[208,768]{1,0:T(8,128)(2,1)}, u32[]{:S(2)}, u32[]{:S(2)}) collective-permute-start(bf16[208,768]{1,0:T(8,128)(2,1)} %get-tuple-element.157), channel_id=1, source_target_pairs={{0,2},{1,3},{2,0},{3,1},{4,6},{5,7},{6,4},{7,5},{8,10},{9,11},{10,... | collective-permute-start | bytes 958472 | tf_op jit(solution)/shard_map/ppermute | solution.py:730
  12.2 10.2 %copy-start.35 = (bf16[192,768]{1,0:T(8,128)(2,1)S(1)}, bf16[192,768]{1,0:T(8,128)(2,1)}, u32[]{:S(2)}) copy-start(bf16[192,768]{1,0:T(8,128)(2,1)} %get-tuple-element.166) | copy-start | bytes 884740
  12.2 9.7 %collective-permute-start.3 = (bf16[208,768]{1,0:T(8,128)(2,1)S(1)}, bf16[208,768]{1,0:T(8,128)(2,1)S(1)}, u32[]{:S(2)}, u32[]{:S(2)}) collective-permute-start(bf16[208,768]{1,0:T(8,128)(2,1)S(1)} %copy-done.31), channel_id=1, source_target_pairs={{0,2},{1,3},{2,0},{3,1},{4,6},{5,7},{6,4},{7,5},{8,10},{9,11},{10,... | collective-permute-start | bytes 958472 | tf_op jit(solution)/shard_map/ppermute | solution.py:730
  16.0 18.5 %copy-start.33 = (bf16[192,768]{1,0:T(8,128)(2,1)S(1)}, bf16[192,768]{1,0:T(8,128)(2,1)}, u32[]{:S(2)}) copy-start(bf16[192,768]{1,0:T(8,128)(2,1)} %get-tuple-element.191) | copy-start | bytes 884740
  16.0 20.0 %copy-start.34 = (bf16[192,768]{1,0:T(8,128)(2,1)S(1)}, bf16[192,768]{1,0:T(8,128)(2,1)}, u32[]{:S(2)}) copy-start(bf16[192,768]{1,0:T(8,128)(2,1)} %get-tuple-element.181) | copy-start | bytes 884740
  16.0 20.5 %copy-start = (bf16[768,768]{1,0:T(8,128)(2,1)S(1)}, bf16[768,768]{1,0:T(8,128)(2,1)}, u32[]{:S(2)}) copy-start(bf16[768,768]{1,0:T(8,128)(2,1)} %refs_5_.1) | copy-start | bytes 3538948
  16.0 9.8 %collective-permute-start.5 = (bf16[208,768]{1,0:T(8,128)(2,1)}, bf16[208,768]{1,0:T(8,128)(2,1)S(1)}, u32[]{:S(2)}, u32[]{:S(2)}) collective-permute-start(bf16[208,768]{1,0:T(8,128)(2,1)} %collective-permute-done.refs_0_), channel_id=1, source_target_pairs={{0,4},{4,0},{8,12},{12,8},{16,20},{20,16},{24,28},{28,24},{1,5},{5... | collective-permute-start | bytes 958472 | tf_op jit(solution)/shard_map/ppermute | solution.py:730
  18.0 9.3 %collective-permute-start.4 = (bf16[208,768]{1,0:T(8,128)(2,1)}, bf16[208,768]{1,0:T(8,128)(2,1)S(1)}, u32[]{:S(2)}, u32[]{:S(2)}) collective-permute-start(bf16[208,768]{1,0:T(8,128)(2,1)} %collective-permute-done.refs_0_), channel_id=1, source_target_pairs={{0,8},{4,12},{8,0},{12,4},{16,24},{20,28},{24,16},{28,20},{1,9},{5... | collective-permute-start | bytes 958472 | tf_op jit(solution)/shard_map/ppermute | solution.py:730
  21.9 11.0 %collective-permute-start.9 = (bf16[208,768]{1,0:T(8,128)(2,1)S(1)}, bf16[208,768]{1,0:T(8,128)(2,1)S(1)}, u32[]{:S(2)}, u32[]{:S(2)}) collective-permute-start(bf16[208,768]{1,0:T(8,128)(2,1)S(1)} %collective-permute-done.3.refs_3_), channel_id=1, source_target_pairs={{0,1},{1,0},{2,3},{3,2},{4,5},{5,4},{6,7},{7,6},{8,9},{9,8},{10,11... | collective-permute-start | bytes 958472 | tf_op jit(solution)/shard_map/ppermute | solution.py:730
  21.9 12.7 %collective-permute-start.6 = (bf16[208,768]{1,0:T(8,128)(2,1)}, bf16[208,768]{1,0:T(8,128)(2,1)S(1)}, u32[]{:S(2)}, u32[]{:S(2)}) collective-permute-start(bf16[208,768]{1,0:T(8,128)(2,1)} %collective-permute-done.refs_0_), channel_id=1, source_target_pairs={{0,1},{1,0},{2,3},{3,2},{4,5},{5,4},{6,7},{7,6},{8,9},{9,8},{10,11... | collective-permute-start | bytes 958472 | tf_op jit(solution)/shard_map/ppermute | solution.py:730
  22.4 8.9 %collective-permute-start.2 = (bf16[192,768]{1,0:T(8,128)(2,1)S(1)}, bf16[192,768]{1,0:T(8,128)(2,1)S(1)}, u32[]{:S(2)}, u32[]{:S(2)}) collective-permute-start(bf16[192,768]{1,0:T(8,128)(2,1)S(1)} %copy-done.35), channel_id=1, source_target_pairs={{0,2},{1,3},{2,0},{3,1},{4,6},{5,7},{6,4},{7,5},{8,10},{9,11},{10,... | collective-permute-start | bytes 884744 | tf_op jit(solution)/shard_map/ppermute | solution.py:730
  25.8 10.2 %collective-permute-start.8 = (bf16[208,768]{1,0:T(8,128)(2,1)S(1)}, bf16[208,768]{1,0:T(8,128)(2,1)S(1)}, u32[]{:S(2)}, u32[]{:S(2)}) collective-permute-start(bf16[208,768]{1,0:T(8,128)(2,1)S(1)} %collective-permute-done.5.refs_2_), channel_id=1, source_target_pairs={{0,1},{1,0},{2,3},{3,2},{4,5},{5,4},{6,7},{7,6},{8,9},{9,8},{10,11... | collective-permute-start | bytes 958472 | tf_op jit(solution)/shard_map/ppermute | solution.py:730
  27.2 9.3 %collective-permute-start.7 = (bf16[208,768]{1,0:T(8,128)(2,1)S(1)}, bf16[208,768]{1,0:T(8,128)(2,1)S(1)}, u32[]{:S(2)}, u32[]{:S(2)}) collective-permute-start(bf16[208,768]{1,0:T(8,128)(2,1)S(1)} %collective-permute-done.4.refs_1_), channel_id=1, source_target_pairs={{0,1},{1,0},{2,3},{3,2},{4,5},{5,4},{6,7},{7,6},{8,9},{9,8},{10,11... | collective-permute-start | bytes 958472 | tf_op jit(solution)/shard_map/ppermute | solution.py:730
  31.3 18.9 %collective-permute-start.13 = (bf16[192,768]{1,0:T(8,128)(2,1)S(1)}, bf16[192,768]{1,0:T(8,128)(2,1)S(1)}, u32[]{:S(2)}, u32[]{:S(2)}) collective-permute-start(bf16[192,768]{1,0:T(8,128)(2,1)S(1)} %collective-permute-done.2.refs_1_), channel_id=1, source_target_pairs={{0,4},{4,0},{8,12},{12,8},{16,20},{20,16},{24,28},{28,24},{1,5},{5... | collective-permute-start | bytes 884744 | tf_op jit(solution)/shard_map/ppermute | solution.py:730
  32.9 7.3 %copy-start.17 = (bf16[768]{0:T(1024)(128)(2,1)S(1)}, bf16[768]{0:T(1024)(128)(2,1)}, u32[]{:S(2)}) copy-start(bf16[768]{0:T(1024)(128)(2,1)} %gain_ref.3) | copy-start | bytes 4612
  32.9 7.3 %copy-start.23 = (bf16[768]{0:T(1024)(128)(2,1)S(1)}, bf16[768]{0:T(1024)(128)(2,1)}, u32[]{:S(2)}) copy-start(bf16[768]{0:T(1024)(128)(2,1)} %bias_ref.1) | copy-start | bytes 4612
  32.9 17.8 %collective-permute-start.12 = (bf16[192,768]{1,0:T(8,128)(2,1)S(1)}, bf16[192,768]{1,0:T(8,128)(2,1)S(1)}, u32[]{:S(2)}, u32[]{:S(2)}) collective-permute-start(bf16[192,768]{1,0:T(8,128)(2,1)S(1)} %collective-permute-done.2.refs_1_), channel_id=1, source_target_pairs={{0,8},{4,12},{8,0},{12,4},{16,24},{20,28},{24,16},{28,20},{1,9},{5... | collective-permute-start | bytes 884744 | tf_op jit(solution)/shard_map/ppermute | solution.py:730
  34.5 14.2 %collective-permute-start.14 = (bf16[192,768]{1,0:T(8,128)(2,1)S(1)}, bf16[192,768]{1,0:T(8,128)(2,1)S(1)}, u32[]{:S(2)}, u32[]{:S(2)}) collective-permute-start(bf16[192,768]{1,0:T(8,128)(2,1)S(1)} %copy-done.33), channel_id=1, source_target_pairs={{0,2},{1,3},{2,0},{3,1},{4,6},{5,7},{6,4},{7,5},{8,10},{9,11},{10,... | collective-permute-start | bytes 884744 | tf_op jit(solution)/shard_map/ppermute | solution.py:730
  36.0 12.7 %collective-permute-start.10 = (bf16[192,768]{1,0:T(8,128)(2,1)S(1)}, bf16[192,768]{1,0:T(8,128)(2,1)S(1)}, u32[]{:S(2)}, u32[]{:S(2)}) collective-permute-start(bf16[192,768]{1,0:T(8,128)(2,1)S(1)} %copy-done.34), channel_id=1, source_target_pairs={{0,2},{1,3},{2,0},{3,1},{4,6},{5,7},{6,4},{7,5},{8,10},{9,11},{10,... | collective-permute-start | bytes 884744 | tf_op jit(solution)/shard_map/ppermute | solution.py:730
  36.6 6.8 %collective-permute-start.11 = (bf16[768,768]{1,0:T(8,128)(2,1)S(1)}, bf16[768,768]{1,0:T(8,128)(2,1)S(1)}, u32[]{:S(2)}, u32[]{:S(2)}) collective-permute-start(bf16[768,768]{1,0:T(8,128)(2,1)S(1)} %copy-done), channel_id=1, source_target_pairs={{0,1},{1,0},{2,3},{3,2},{4,5},{5,4},{6,7},{7,6},{8,9},{9,8},{10,11... | collective-permute-start | bytes 3538952 | tf_op jit(solution)/shard_map/ppermute | solution.py:730
  43.3 23.1 %copy-start.4 = (f32[512,768]{1,0:T(8,128)}, f32[512,768]{1,0:T(8,128)S(1)}, u32[]{:S(2)}) copy-start(f32[512,768]{1,0:T(8,128)S(1)} %get-tuple-element.222.z_ref) | copy-start | bytes 4718596
  43.3 16.8 %collective-permute-start.15 = (bf16[768,768]{1,0:T(8,128)(2,1)S(1)}, bf16[768,768]{1,0:T(8,128)(2,1)S(1)}, u32[]{:S(2)}, u32[]{:S(2)}) collective-permute-start(bf16[768,768]{1,0:T(8,128)(2,1)S(1)} %copy-done.2), channel_id=1, source_target_pairs={{0,1},{1,0},{2,3},{3,2},{4,5},{5,4},{6,7},{7,6},{8,9},{9,8},{10,11... | collective-permute-start | bytes 3538952 | tf_op jit(solution)/shard_map/ppermute | solution.py:730
  47.4 13.2 %copy-start.26 = (bf16[512,768]{1,0:T(8,128)(2,1)}, bf16[512,768]{1,0:T(8,128)(2,1)S(1)}, u32[]{:S(2)}) copy-start(bf16[512,768]{1,0:T(8,128)(2,1)S(1)} %get-tuple-element.193.refs_0_.act_b) | copy-start | bytes 2359300
  48.7 15.4 %collective-permute-start.20 = (bf16[192,768]{1,0:T(8,128)(2,1)S(1)}, bf16[192,768]{1,0:T(8,128)(2,1)S(1)}, u32[]{:S(2)}, u32[]{:S(2)}) collective-permute-start(bf16[192,768]{1,0:T(8,128)(2,1)S(1)} %collective-permute-done.10.refs_2_), channel_id=1, source_target_pairs={{0,1},{1,0},{2,3},{3,2},{4,5},{5,4},{6,7},{7,6},{8,9},{9,8},{10,11... | collective-permute-start | bytes 884744 | tf_op jit(solution)/shard_map/ppermute | solution.py:730
  48.7 10.8 %collective-permute-start.18 = (bf16[192,768]{1,0:T(8,128)(2,1)S(1)}, bf16[192,768]{1,0:T(8,128)(2,1)S(1)}, u32[]{:S(2)}, u32[]{:S(2)}) collective-permute-start(bf16[192,768]{1,0:T(8,128)(2,1)S(1)} %collective-permute-done.10.refs_2_), channel_id=1, source_target_pairs={{0,4},{4,0},{8,12},{12,8},{16,20},{20,16},{24,28},{28,24},{1,5},{5... | collective-permute-start | bytes 884744 | tf_op jit(solution)/shard_map/ppermute | solution.py:730
  50.2 9.8 %collective-permute-start.17 = (bf16[192,768]{1,0:T(8,128)(2,1)S(1)}, bf16[192,768]{1,0:T(8,128)(2,1)S(1)}, u32[]{:S(2)}, u32[]{:S(2)}) collective-permute-start(bf16[192,768]{1,0:T(8,128)(2,1)S(1)} %collective-permute-done.10.refs_2_), channel_id=1, source_target_pairs={{0,8},{4,12},{8,0},{12,4},{16,24},{20,28},{24,16},{28,20},{1,9},{5... | collective-permute-start | bytes 884744 | tf_op jit(solution)/shard_map/ppermute | solution.py:730
  50.7 8.9 %collective-permute-start.19 = (bf16[192,768]{1,0:T(8,128)(2,1)S(1)}, bf16[192,768]{1,0:T(8,128)(2,1)S(1)}, u32[]{:S(2)}, u32[]{:S(2)}) collective-permute-start(bf16[192,768]{1,0:T(8,128)(2,1)S(1)} %copy-done.32), channel_id=1, source_target_pairs={{0,2},{1,3},{2,0},{3,1},{4,6},{5,7},{6,4},{7,5},{8,10},{9,11},{10,... | collective-permute-start | bytes 884744 | tf_op jit(solution)/shard_map/ppermute | solution.py:730
  53.9 8.1 %copy-start.8 = (bf16[768,768]{1,0:T(8,128)(2,1)}, bf16[768,768]{1,0:T(8,128)(2,1)S(1)}, u32[]{:S(2)}) copy-start(bf16[768,768]{1,0:T(8,128)(2,1)S(1)} %get-tuple-element.198.refs_2_) | copy-start | bytes 3538948
  59.6 2.8 %collective-permute-start.16 = (bf16[768,768]{1,0:T(8,128)(2,1)S(1)}, bf16[768,768]{1,0:T(8,128)(2,1)S(1)}, u32[]{:S(2)}, u32[]{:S(2)}) collective-permute-start(bf16[768,768]{1,0:T(8,128)(2,1)S(1)} %get-tuple-element.198.refs_2_), channel_id=1, source_target_pairs={{0,1},{1,0},{2,3},{3,2},{4,5},{5,4},{6,7},{7,6},{8,9},{9,8},{10,11... | collective-permute-start | bytes 3538952 | tf_op jit(solution)/shard_map/ppermute | solution.py:730
  59.6 4.6 %collective-permute-start.23 = (bf16[192,768]{1,0:T(8,128)(2,1)S(1)}, bf16[192,768]{1,0:T(8,128)(2,1)S(1)}, u32[]{:S(2)}, u32[]{:S(2)}) collective-permute-start(bf16[192,768]{1,0:T(8,128)(2,1)S(1)} %collective-permute-done.19.refs_5_), channel_id=1, source_target_pairs={{0,1},{1,0},{2,3},{3,2},{4,5},{5,4},{6,7},{7,6},{8,9},{9,8},{10,11... | collective-permute-start | bytes 884744 | tf_op jit(solution)/shard_map/ppermute | solution.py:730
  60.1 4.1 %collective-permute-start.22 = (bf16[192,768]{1,0:T(8,128)(2,1)S(1)}, bf16[192,768]{1,0:T(8,128)(2,1)S(1)}, u32[]{:S(2)}, u32[]{:S(2)}) collective-permute-start(bf16[192,768]{1,0:T(8,128)(2,1)S(1)} %collective-permute-done.18.refs_4_), channel_id=1, source_target_pairs={{0,1},{1,0},{2,3},{3,2},{4,5},{5,4},{6,7},{7,6},{8,9},{9,8},{10,11... | collective-permute-start | bytes 884744 | tf_op jit(solution)/shard_map/ppermute | solution.py:730
  60.1 4.0 %collective-permute-start.21 = (bf16[192,768]{1,0:T(8,128)(2,1)S(1)}, bf16[192,768]{1,0:T(8,128)(2,1)S(1)}, u32[]{:S(2)}, u32[]{:S(2)}) collective-permute-start(bf16[192,768]{1,0:T(8,128)(2,1)S(1)} %collective-permute-done.17.refs_3_), channel_id=1, source_target_pairs={{0,1},{1,0},{2,3},{3,2},{4,5},{5,4},{6,7},{7,6},{8,9},{9,8},{10,11... | collective-permute-start | bytes 884744 | tf_op jit(solution)/shard_map/ppermute | solution.py:730
  70.9 5.8 %collective-permute-start.24 = (bf16[8,192,768]{2,1,0:T(8,128)(2,1)S(1)}, bf16[8,192,768]{2,1,0:T(8,128)(2,1)S(1)}, u32[]{:S(2)}, u32[]{:S(2)}) collective-permute-start(bf16[8,192,768]{2,1,0:T(8,128)(2,1)S(1)} %down_back.2), channel_id=1, source_target_pairs={{0,1},{1,0},{2,3},{3,2},{4,5},{5,4},{6,7},{7,6},{8,9},{9,8},{10,11... | collective-permute-start | bytes 7077896 | tf_op jit(solution)/shard_map/ppermute | solution.py:730
  76.3 4.6 %collective-permute-start.25 = (bf16[8,192,768]{2,1,0:T(8,128)(2,1)S(1)}, bf16[8,192,768]{2,1,0:T(8,128)(2,1)S(1)}, u32[]{:S(2)}, u32[]{:S(2)}) collective-permute-start(bf16[8,192,768]{2,1,0:T(8,128)(2,1)S(1)} %get-tuple-element.220), channel_id=1, source_target_pairs={{0,1},{1,0},{2,3},{3,2},{4,5},{5,4},{6,7},{7,6},{8,9},{9,8},{10,11... | collective-permute-start | bytes 7077896 | tf_op jit(solution)/shard_map/ppermute | solution.py:730
  78.7 34.6 %collective-permute-start.26 = (bf16[4,192,768]{2,1,0:T(8,128)(2,1)S(1)}, bf16[4,192,768]{2,1,0:T(8,128)(2,1)S(1)}, u32[]{:S(2)}, u32[]{:S(2)}) collective-permute-start(bf16[4,192,768]{2,1,0:T(8,128)(2,1)S(1)} %get-tuple-element.215), channel_id=1, source_target_pairs={{0,2},{1,3},{2,0},{3,1},{4,6},{5,7},{6,4},{7,5},{8,10},{9,11},{10,... | collective-permute-start | bytes 3538952 | tf_op jit(solution)/shard_map/ppermute | solution.py:730
  96.4 15.7 %collective-permute-start.27 = (bf16[2,192,768]{2,1,0:T(8,128)(2,1)S(1)}, bf16[2,192,768]{2,1,0:T(8,128)(2,1)S(1)}, u32[]{:S(2)}, u32[]{:S(2)}) collective-permute-start(bf16[2,192,768]{2,1,0:T(8,128)(2,1)S(1)} %get-tuple-element.243), channel_id=1, source_target_pairs={{0,8},{4,12},{8,0},{12,4},{16,24},{20,28},{24,16},{28,20},{1,9},{5... | collective-permute-start | bytes 1769480 | tf_op jit(solution)/shard_map/ppermute | solution.py:730
  98.1 15.3 %collective-permute-start.28 = (bf16[2,192,768]{2,1,0:T(8,128)(2,1)S(1)}, bf16[2,192,768]{2,1,0:T(8,128)(2,1)S(1)}, u32[]{:S(2)}, u32[]{:S(2)}) collective-permute-start(bf16[2,192,768]{2,1,0:T(8,128)(2,1)S(1)} %get-tuple-element.245), channel_id=1, source_target_pairs={{0,4},{4,0},{8,12},{12,8},{16,20},{20,16},{24,28},{28,24},{1,5},{5... | collective-permute-start | bytes 1769480 | tf_op jit(solution)/shard_map/ppermute | solution.py:730
  111.6 4.9 %collective-permute-start.29 = (bf16[8,208,768]{2,1,0:T(8,128)(2,1)S(1)}, bf16[8,208,768]{2,1,0:T(8,128)(2,1)S(1)}, u32[]{:S(2)}, u32[]{:S(2)}) collective-permute-start(bf16[8,208,768]{2,1,0:T(8,128)(2,1)S(1)} %copy-done.29), channel_id=1, source_target_pairs={{0,1},{1,0},{2,3},{3,2},{4,5},{5,4},{6,7},{7,6},{8,9},{9,8},{10,11... | collective-permute-start | bytes 7667720 | tf_op jit(solution)/shard_map/ppermute | solution.py:730
  113.8 20.9 %collective-permute-start.32 = (bf16[2,192,768]{2,1,0:T(8,128)(2,1)S(1)}, bf16[2,192,768]{2,1,0:T(8,128)(2,1)S(1)}, u32[]{:S(2)}, u32[]{:S(2)}) collective-permute-start(bf16[2,192,768]{2,1,0:T(8,128)(2,1)S(1)} %get-tuple-element.246), channel_id=1, source_target_pairs={{0,4},{4,0},{8,12},{12,8},{16,20},{20,16},{24,28},{28,24},{1,5},{5... | collective-permute-start | bytes 1769480 | tf_op jit(solution)/shard_map/ppermute | solution.py:730
  114.4 20.2 %collective-permute-start.30 = (bf16[192,768]{1,0:T(8,128)(2,1)S(1)}, bf16[192,768]{1,0:T(8,128)(2,1)S(1)}, u32[]{:S(2)}, u32[]{:S(2)}) collective-permute-start(bf16[192,768]{1,0:T(8,128)(2,1)S(1)} %get-tuple-element.263), channel_id=1, source_target_pairs={{0,4},{4,0},{8,12},{12,8},{16,20},{20,16},{24,28},{28,24},{1,5},{5... | collective-permute-start | bytes 884744 | tf_op jit(solution)/shard_map/ppermute | solution.py:730
  115.9 18.8 %collective-permute-start.31 = (bf16[192,768]{1,0:T(8,128)(2,1)S(1)}, bf16[192,768]{1,0:T(8,128)(2,1)S(1)}, u32[]{:S(2)}, u32[]{:S(2)}) collective-permute-start(bf16[192,768]{1,0:T(8,128)(2,1)S(1)} %get-tuple-element.264), channel_id=1, source_target_pairs={{0,8},{4,12},{8,0},{12,4},{16,24},{20,28},{24,16},{28,20},{1,9},{5... | collective-permute-start | bytes 884744 | tf_op jit(solution)/shard_map/ppermute | solution.py:730
  122.4 24.5 %collective-permute-start.34 = (bf16[3,208,768]{2,1,0:T(8,128)(2,1)}, bf16[3,208,768]{2,1,0:T(8,128)(2,1)S(1)}, u32[]{:S(2)}, u32[]{:S(2)}) collective-permute-start(bf16[3,208,768]{2,1,0:T(8,128)(2,1)} %get-tuple-element.273), channel_id=1, source_target_pairs={{0,2},{1,3},{2,0},{3,1},{4,6},{5,7},{6,4},{7,5},{8,10},{9,11},{10,... | collective-permute-start | bytes 2875400 | tf_op jit(solution)/shard_map/ppermute | solution.py:730
  135.0 8.8 %collective-permute-start.33 = (bf16[192,768]{1,0:T(8,128)(2,1)S(1)}, bf16[192,768]{1,0:T(8,128)(2,1)S(1)}, u32[]{:S(2)}, u32[]{:S(2)}) collective-permute-start(bf16[192,768]{1,0:T(8,128)(2,1)S(1)} %get-tuple-element.270), channel_id=1, source_target_pairs={{0,8},{4,12},{8,0},{12,4},{16,24},{20,28},{24,16},{28,20},{1,9},{5... | collective-permute-start | bytes 884744 | tf_op jit(solution)/shard_map/ppermute | solution.py:730
  136.5 16.6 %collective-permute-start.35 = (bf16[192,768]{1,0:T(8,128)(2,1)S(1)}, bf16[192,768]{1,0:T(8,128)(2,1)S(1)}, u32[]{:S(2)}, u32[]{:S(2)}) collective-permute-start(bf16[192,768]{1,0:T(8,128)(2,1)S(1)} %get-tuple-element.268), channel_id=1, source_target_pairs={{0,2},{1,3},{2,0},{3,1},{4,6},{5,7},{6,4},{7,5},{8,10},{9,11},{10,... | collective-permute-start | bytes 884744 | tf_op jit(solution)/shard_map/ppermute | solution.py:730
  137.2 9.8 %copy-start.25 = (bf16[4,208,768]{2,1,0:T(8,128)(2,1)S(1)}, bf16[4,208,768]{2,1,0:T(8,128)(2,1)}, u32[]{:S(2)}) copy-start(bf16[4,208,768]{2,1,0:T(8,128)(2,1)} %get-tuple-element.277.refs_0_) | copy-start | bytes 3833860
  137.2 24.2 %collective-permute-start.38 = (bf16[208,768]{1,0:T(8,128)(2,1)S(1)}, bf16[208,768]{1,0:T(8,128)(2,1)S(1)}, u32[]{:S(2)}, u32[]{:S(2)}) collective-permute-start(bf16[208,768]{1,0:T(8,128)(2,1)S(1)} %copy-done.30), channel_id=1, source_target_pairs={{0,2},{1,3},{2,0},{3,1},{4,6},{5,7},{6,4},{7,5},{8,10},{9,11},{10,... | collective-permute-start | bytes 958472 | tf_op jit(solution)/shard_map/ppermute | solution.py:730
  143.9 14.6 %collective-permute-start.36 = (bf16[192,768]{1,0:T(8,128)(2,1)S(1)}, bf16[192,768]{1,0:T(8,128)(2,1)S(1)}, u32[]{:S(2)}, u32[]{:S(2)}) collective-permute-start(bf16[192,768]{1,0:T(8,128)(2,1)S(1)} %add.19.refs_0_), channel_id=1, source_target_pairs={{0,16},{4,20},{8,24},{12,28},{16,0},{20,4},{24,8},{28,12},{1,17},{... | collective-permute-start | bytes 884744 | tf_op jit(solution)/shard_map/ppermute | solution.py:730
  147.1 14.3 %collective-permute-start.39 = (bf16[208,768]{1,0:T(8,128)(2,1)S(1)}, bf16[208,768]{1,0:T(8,128)(2,1)S(1)}, u32[]{:S(2)}, u32[]{:S(2)}) collective-permute-start(bf16[208,768]{1,0:T(8,128)(2,1)S(1)} %get-tuple-element.280), channel_id=1, source_target_pairs={{0,4},{4,0},{8,12},{12,8},{16,20},{20,16},{24,28},{28,24},{1,5},{5... | collective-permute-start | bytes 958472 | tf_op jit(solution)/shard_map/ppermute | solution.py:730
  148.5 13.3 %collective-permute-start.37 = (bf16[208,768]{1,0:T(8,128)(2,1)S(1)}, bf16[208,768]{1,0:T(8,128)(2,1)S(1)}, u32[]{:S(2)}, u32[]{:S(2)}) collective-permute-start(bf16[208,768]{1,0:T(8,128)(2,1)S(1)} %get-tuple-element.274), channel_id=1, source_target_pairs={{0,4},{4,0},{8,12},{12,8},{16,20},{20,16},{24,28},{28,24},{1,5},{5... | collective-permute-start | bytes 958472 | tf_op jit(solution)/shard_map/ppermute | solution.py:730
  158.6 16.3 %collective-permute-start.40 = (bf16[192,768]{1,0:T(8,128)(2,1)S(1)}, bf16[192,768]{1,0:T(8,128)(2,1)S(1)}, u32[]{:S(2)}, u32[]{:S(2)}) collective-permute-start(bf16[192,768]{1,0:T(8,128)(2,1)S(1)} %add.22.refs_0_), channel_id=1, source_target_pairs={{0,8},{4,12},{8,0},{12,4},{16,24},{20,28},{24,16},{28,20},{1,9},{5... | collective-permute-start | bytes 884744 | tf_op jit(solution)/shard_map/ppermute | solution.py:730
  158.7 18.2 %collective-permute-start.41 = (bf16[192,768]{1,0:T(8,128)(2,1)S(1)}, bf16[192,768]{1,0:T(8,128)(2,1)S(1)}, u32[]{:S(2)}, u32[]{:S(2)}) collective-permute-start(bf16[192,768]{1,0:T(8,128)(2,1)S(1)} %add.21.refs_0_), channel_id=1, source_target_pairs={{0,16},{4,20},{8,24},{12,28},{16,0},{20,4},{24,8},{28,12},{1,17},{... | collective-permute-start | bytes 884744 | tf_op jit(solution)/shard_map/ppermute | solution.py:730
  162.0 18.7 %collective-permute-start.42 = (bf16[208,768]{1,0:T(8,128)(2,1)S(1)}, bf16[208,768]{1,0:T(8,128)(2,1)S(1)}, u32[]{:S(2)}, u32[]{:S(2)}) collective-permute-start(bf16[208,768]{1,0:T(8,128)(2,1)S(1)} %get-tuple-element.282), channel_id=1, source_target_pairs={{0,8},{4,12},{8,0},{12,4},{16,24},{20,28},{24,16},{28,20},{1,9},{5... | collective-permute-start | bytes 958472 | tf_op jit(solution)/shard_map/ppermute | solution.py:730
  162.3 22.7 %collective-permute-start.45 = (bf16[192,768]{1,0:T(8,128)(2,1)S(1)}, bf16[192,768]{1,0:T(8,128)(2,1)S(1)}, u32[]{:S(2)}, u32[]{:S(2)}) collective-permute-start(bf16[192,768]{1,0:T(8,128)(2,1)S(1)} %add.22.refs_0_), channel_id=1, source_target_pairs={{0,4},{4,0},{8,12},{12,8},{16,20},{20,16},{24,28},{28,24},{1,5},{5... | collective-permute-start | bytes 884744 | tf_op jit(solution)/shard_map/ppermute | solution.py:730
  174.9 10.1 %collective-permute-start.46 = (bf16[192,768]{1,0:T(8,128)(2,1)S(1)}, bf16[192,768]{1,0:T(8,128)(2,1)S(1)}, u32[]{:S(2)}, u32[]{:S(2)}) collective-permute-start(bf16[192,768]{1,0:T(8,128)(2,1)S(1)} %collective-permute-done.40.refs_1_), channel_id=1, source_target_pairs={{0,4},{4,0},{8,12},{12,8},{16,20},{20,16},{24,28},{28,24},{1,5},{5... | collective-permute-start | bytes 884744 | tf_op jit(solution)/shard_map/ppermute | solution.py:730
  180.8 16.4 %collective-permute-start.47 = (bf16[208,768]{1,0:T(8,128)(2,1)S(1)}, bf16[208,768]{1,0:T(8,128)(2,1)S(1)}, u32[]{:S(2)}, u32[]{:S(2)}) collective-permute-start(bf16[208,768]{1,0:T(8,128)(2,1)S(1)} %add.25.refs_0_), channel_id=1, source_target_pairs={{0,16},{4,20},{8,24},{12,28},{16,0},{20,4},{24,8},{28,12},{1,17},{... | collective-permute-start | bytes 958472 | tf_op jit(solution)/shard_map/ppermute | solution.py:730
  180.9 12.8 %collective-permute-start.44 = (bf16[192,768]{1,0:T(8,128)(2,1)S(1)}, bf16[192,768]{1,0:T(8,128)(2,1)S(1)}, u32[]{:S(2)}, u32[]{:S(2)}) collective-permute-start(bf16[192,768]{1,0:T(8,128)(2,1)S(1)} %add.24.refs_0_), channel_id=1, source_target_pairs={{0,8},{4,12},{8,0},{12,4},{16,24},{20,28},{24,16},{28,20},{1,9},{5... | collective-permute-start | bytes 884744 | tf_op jit(solution)/shard_map/ppermute | solution.py:730
  181.6 12.1 %collective-permute-start.43 = (bf16[192,768]{1,0:T(8,128)(2,1)S(1)}, bf16[192,768]{1,0:T(8,128)(2,1)S(1)}, u32[]{:S(2)}, u32[]{:S(2)}) collective-permute-start(bf16[192,768]{1,0:T(8,128)(2,1)S(1)} %add.24.refs_0_), channel_id=1, source_target_pairs={{0,4},{4,0},{8,12},{12,8},{16,20},{20,16},{24,28},{28,24},{1,5},{5... | collective-permute-start | bytes 884744 | tf_op jit(solution)/shard_map/ppermute | solution.py:730
  197.3 9.4 %collective-permute-start.49 = (bf16[208,768]{1,0:T(8,128)(2,1)S(1)}, bf16[208,768]{1,0:T(8,128)(2,1)S(1)}, u32[]{:S(2)}, u32[]{:S(2)}) collective-permute-start(bf16[208,768]{1,0:T(8,128)(2,1)S(1)} %add.26.refs_0_), channel_id=1, source_target_pairs={{0,8},{4,12},{8,0},{12,4},{16,24},{20,28},{24,16},{28,20},{1,9},{5... | collective-permute-start | bytes 958472 | tf_op jit(solution)/shard_map/ppermute | solution.py:730
  197.4 11.3 %collective-permute-start.48 = (bf16[192,768]{1,0:T(8,128)(2,1)S(1)}, bf16[192,768]{1,0:T(8,128)(2,1)S(1)}, u32[]{:S(2)}, u32[]{:S(2)}) collective-permute-start(bf16[192,768]{1,0:T(8,128)(2,1)S(1)} %collective-permute-done.44.refs_1_), channel_id=1, source_target_pairs={{0,4},{4,0},{8,12},{12,8},{16,20},{20,16},{24,28},{28,24},{1,5},{5... | collective-permute-start | bytes 884744 | tf_op jit(solution)/shard_map/ppermute | solution.py:730
  199.5 14.7 %collective-permute-start.50 = (bf16[208,768]{1,0:T(8,128)(2,1)S(1)}, bf16[208,768]{1,0:T(8,128)(2,1)S(1)}, u32[]{:S(2)}, u32[]{:S(2)}) collective-permute-start(bf16[208,768]{1,0:T(8,128)(2,1)S(1)} %add.26.refs_0_), channel_id=1, source_target_pairs={{0,4},{4,0},{8,12},{12,8},{16,20},{20,16},{24,28},{28,24},{1,5},{5... | collective-permute-start | bytes 958472 | tf_op jit(solution)/shard_map/ppermute | solution.py:730
  206.8 13.5 %collective-permute-start.51 = (bf16[208,768]{1,0:T(8,128)(2,1)S(1)}, bf16[208,768]{1,0:T(8,128)(2,1)S(1)}, u32[]{:S(2)}, u32[]{:S(2)}) collective-permute-start(bf16[208,768]{1,0:T(8,128)(2,1)S(1)} %collective-permute-done.49.refs_1_), channel_id=1, source_target_pairs={{0,4},{4,0},{8,12},{12,8},{16,20},{20,16},{24,28},{28,24},{1,5},{5... | collective-permute-start | bytes 958472 | tf_op jit(solution)/shard_map/ppermute | solution.py:730
  (24 other events, 93.2 us)
